TPU v7x, 256 devices: a whole 4x4x8 slice. The times are simulated.
256 devices in a mesh: head: 16 (over x, y_lo, core), ctx: 16 (over y_hi, z).
Axes of the slice: x: 4, y: 4 (y_hi: 2, y_lo: 2; y = y_hi * 2 + y_lo), z: 8, core: 2. Of those that a mesh axis runs over, the one named last changes fastest.
Arguments:
- queries: bfloat16 [4, 16, 256, 12288], P(None, 'ctx', 'head'), may hold values from -5 to 5
- key_vectors: bfloat16 [4, 16, 256, 1024], P(None, 'ctx', 'head'), may hold values from -5 to 5
- value_vectors: bfloat16 [4, 16, 256, 1024], P(None, 'ctx', 'head'), may hold values from -6 to 6
- grad_output: bfloat16 [4, 16, 256, 12288], P(None, 'ctx', 'head'), may hold values from -6 to 6
- doc_ids: int32 [16384], replicated, may hold values from 0 to 31, never falling along the last dimension, each value on 1 to 1024 neighbouring positions
Outputs:
- grad_queries: bfloat16 [4, 16, 256, 12288], P(None, 'ctx', 'head')
- grad_keys: bfloat16 [4, 16, 256, 1024], P(None, 'ctx', 'head')
- grad_values: bfloat16 [4, 16, 256, 1024], P(None, 'ctx', 'head')
Inputs may be any that keep to these rules, and one draw needn't show every extreme that they name: `doc_ids`: document numbers never fall along the sequence; a document holds 1 to 1024 tokens.
All inputs are finite; a program needn't handle non-finite values.
Results may differ from a plain program's by a relative error of at most 0.0066.
Values may be sent and summed in bfloat16 or wider, within the bound.
A program may use at most 128 MiB of HBM per device.

v0:
```python
import math

import jax
import jax.numpy as jnp
from jax import lax
from jax.sharding import PartitionSpec as P

HD = 128


def passed_along(x, axis, by):
    peers = lax.axis_size(axis)
    return lax.ppermute(x, axis, [(i, (i + by) % peers) for i in range(peers)])


def slot_grads(query_rows, grad_rows, key_rows, value_rows, allowed, factor):
    scores = (
        jnp.einsum("hqd,kd->hqk", query_rows, key_rows, preferred_element_type=jnp.float32) * factor
    )
    masked = jnp.where(allowed[None], scores, -jnp.inf)
    row_max = jnp.max(masked, axis=-1, keepdims=True)
    exponent = jnp.where(allowed[None], jnp.exp(masked - row_max), 0.0)
    weights = exponent / jnp.sum(exponent, axis=-1, keepdims=True)
    dweights = jnp.einsum("hqd,kd->hqk", grad_rows, value_rows, preferred_element_type=jnp.float32)
    row_dot = jnp.sum(weights * dweights, axis=-1, keepdims=True)
    dscores = (factor * weights * (dweights - row_dot)).astype(jnp.bfloat16)
    weight_bf = weights.astype(jnp.bfloat16)
    grad_q = jnp.einsum(
        "hqk,kd->hqd", dscores, key_rows, preferred_element_type=jnp.float32
    ).astype(jnp.bfloat16)
    grad_k = jnp.einsum("hqk,hqd->kd", dscores, query_rows, preferred_element_type=jnp.float32)
    grad_v = jnp.einsum("hqk,hqd->kd", weight_bf, grad_rows, preferred_element_type=jnp.float32)
    return (grad_q, grad_k, grad_v)


def body(queries, key_vectors, value_vectors, grad_output, doc_ids):
    head_count = lax.axis_size("head")
    ctx_count = lax.axis_size("ctx")
    ctx_at = lax.axis_index("ctx")
    slot_count, _, in_rows, q_width = queries.shape
    kv_width = key_vectors.shape[3]
    stripe = in_rows * head_count
    local_heads = q_width // (head_count * HD)
    factor = 1.0 / math.sqrt(HD)

    def duplicate(tensor):
        tensor = tensor.reshape(slot_count, 1, in_rows, kv_width // HD, 1, HD)
        tensor = jnp.broadcast_to(tensor, (slot_count, 1, in_rows, kv_width // HD, 2, HD))
        return tensor.reshape(slot_count, 1, in_rows, 2 * kv_width)

    key_send = duplicate(key_vectors)
    value_send = duplicate(value_vectors)
    query_local, key_local, value_local, grad_local = (
        lax.all_to_all(queries, "head", split_axis=3, concat_axis=2, tiled=True),
        lax.all_to_all(key_send, "head", split_axis=3, concat_axis=2, tiled=True),
        lax.all_to_all(value_send, "head", split_axis=3, concat_axis=2, tiled=True),
        lax.all_to_all(grad_output, "head", split_axis=3, concat_axis=2, tiled=True),
    )
    paired = jnp.stack([key_local, value_local]).reshape(2, slot_count, stripe, -1)
    near_kv = passed_along(paired, "ctx", 1)
    far_kv = passed_along(near_kv, "ctx", 1)
    doc_pad = jnp.concatenate([jnp.full((2 * stripe,), -1, jnp.int32), doc_ids])
    offsets = jnp.arange(stripe, dtype=jnp.int32)
    key_offsets = jnp.arange(3 * stripe, dtype=jnp.int32)
    query_all = query_local.reshape(slot_count, stripe, local_heads, HD).transpose(0, 2, 1, 3)
    grad_all = grad_local.reshape(slot_count, stripe, local_heads, HD).transpose(0, 2, 1, 3)
    near_back = (ctx_at < 1).astype(jnp.int32)
    far_back = (ctx_at < 2).astype(jnp.int32)

    def visit_slot(inputs):
        query_rows, grad_rows, slot_at = inputs
        near_slot = jnp.maximum(slot_at - near_back, 0)
        far_slot = jnp.maximum(slot_at - far_back, 0)
        window_kv = jnp.concatenate(
            [
                lax.dynamic_index_in_dim(far_kv, far_slot, 1, keepdims=False),
                lax.dynamic_index_in_dim(near_kv, near_slot, 1, keepdims=False),
                lax.dynamic_index_in_dim(paired, slot_at, 1, keepdims=False),
            ],
            axis=1,
        )
        stripe_at = slot_at * ctx_count + ctx_at
        query_pos = stripe_at * stripe + offsets
        key_pos = (stripe_at - 2) * stripe + key_offsets
        query_doc = lax.dynamic_slice_in_dim(doc_ids, stripe_at * stripe, stripe)
        key_doc = lax.dynamic_slice_in_dim(doc_pad, stripe_at * stripe, 3 * stripe)
        distance = query_pos[:, None] - key_pos[None, :]
        allowed = (
            (distance >= 0)
            & (distance < 2 * stripe)
            & (key_pos[None, :] >= 0)
            & (query_doc[:, None] == key_doc[None, :])
        )
        grad_q, grad_k, grad_v = slot_grads(
            query_rows, grad_rows, window_kv[0], window_kv[1], allowed, factor
        )
        return (grad_q, jnp.stack([grad_k, grad_v]).reshape(2, 3, stripe, HD))

    grad_q, pieces = lax.map(
        visit_slot, (query_all, grad_all, jnp.arange(slot_count, dtype=jnp.int32))
    )

    def restored(block, hops):
        return jnp.where(ctx_at < hops, jnp.roll(block, -1, axis=0), block)

    far_part = restored(pieces[:, :, 0], 2)
    near_part = restored(pieces[:, :, 1], 1)
    own_part = pieces[:, :, 2]
    first_hop = passed_along(far_part, "ctx", -1)
    collected = own_part + passed_along(first_hop + near_part, "ctx", -1)
    halved = collected.astype(jnp.bfloat16)
    query_send = grad_q.transpose(0, 2, 1, 3).reshape(slot_count, 1, stripe, local_heads * HD)
    key_back = halved[:, 0].reshape(slot_count, 1, stripe, HD)
    value_back = halved[:, 1].reshape(slot_count, 1, stripe, HD)
    grad_queries, key_home, value_home = (
        lax.all_to_all(query_send, "head", split_axis=2, concat_axis=3, tiled=True),
        lax.all_to_all(key_back, "head", split_axis=2, concat_axis=3, tiled=True),
        lax.all_to_all(value_back, "head", split_axis=2, concat_axis=3, tiled=True),
    )

    def fold_pairs(tensor):
        tensor = tensor.reshape(slot_count, 1, in_rows, kv_width // HD, 2, HD).astype(jnp.float32)
        return (
            jnp.sum(tensor, axis=4).astype(jnp.bfloat16).reshape(slot_count, 1, in_rows, kv_width)
        )

    grad_keys = fold_pairs(key_home)
    grad_values = fold_pairs(value_home)
    return (grad_queries, grad_keys, grad_values)


def solution(mesh):
    placed = (
        P(None, "ctx", "head", None),
        P(None, "ctx", "head", None),
        P(None, "ctx", "head", None),
        P(None, "ctx", "head", None),
        P(),
    )
    return jax.shard_map(
        body,
        mesh=mesh,
        in_specs=placed,
        out_specs=(
            P(None, "ctx", "head", None),
            P(None, "ctx", "head", None),
            P(None, "ctx", "head", None),
        ),
        check_vma=False,
    )
```

profile of v0, /device:TPU:1, one launch (start us, length us, event | category | flops | bytes accessed | tf_op | source)
XLA Modules:
  0.0 451.2 jit_solution(4438567535131148367)
XLA Ops:
  3.0 2.8 reshape.198
  5.8 6.8 %all-to-all-start.2 = ((bf16[16,2,4096]{2,1,0:T(2,128)(2,1)}), bf16[16,2,4096]{2,1,0:T(2,128)(2,1)S(1)}, u32[]{:S(2)}, u32[]{:S(2)}) async-start(bf16[16,2,4096]{2,1,0:T(2,128)(2,1)} %reshape.198), calls=%async_computation.2 | async-start | bytes 524288 | tf_op jit(solution)/shard_map/all_to_all | solution.py:56
  14.2 2.8 reshape.200
  17.0 3.1 all-to-all-done.2
  20.0 3.7 all-to-all-start.1
  23.8 15.0 %copy.120 = bf16[4,1,16,12288]{2,0,1,3:T(4,128)(2,1)} copy(bf16[4,1,16,12288]{3,2,1,0:T(8,128)(2,1)} %param.7) | data formatting | bytes 3145728 | tf_op args[0]
  38.7 17.8 %reshape.196 = bf16[16,2,24576]{2,1,0:T(2,128)(2,1)} reshape(bf16[12288,1,4,16]{3,2,1,0:T(4,128)(2,1)} %bitcast.208) | data formatting | bytes 3145728
  57.2 5.8 %all-to-all-start = ((bf16[16,2,24576]{2,1,0:T(2,128)(2,1)}), bf16[16,2,24576]{2,1,0:T(2,128)(2,1)S(1)}, u32[]{:S(2)}, u32[]{:S(2)}) async-start(bf16[16,2,24576]{2,1,0:T(2,128)(2,1)} %reshape.196), calls=%async_computation | async-start | bytes 3145728 | tf_op jit(solution)/shard_map/all_to_all | solution.py:54
  63.0 12.1 %copy.129 = bf16[4,1,16,12288]{2,0,1,3:T(4,128)(2,1)} copy(bf16[4,1,16,12288]{3,2,1,0:T(8,128)(2,1)S(1)} %copy-done.4) | data formatting | bytes 3145728 | tf_op args[3]
  75.1 17.7 %reshape.202 = bf16[16,2,24576]{2,1,0:T(2,128)(2,1)} reshape(bf16[12288,1,4,16]{3,2,1,0:T(4,128)(2,1)} %bitcast.209) | data formatting | bytes 3145728
  93.9 5.7 %all-to-all-start.3 = ((bf16[16,2,24576]{2,1,0:T(2,128)(2,1)}), bf16[16,2,24576]{2,1,0:T(2,128)(2,1)}, u32[]{:S(2)}, u32[]{:S(2)}) async-start(bf16[16,2,24576]{2,1,0:T(2,128)(2,1)} %reshape.202), calls=%async_computation.3 | async-start | bytes 3145728 | tf_op jit(solution)/shard_map/all_to_all | solution.py:57
  106.7 25.9 %collective-permute-done = bf16[2,4,256,128]{3,2,1,0:T(8,128)(2,1)} collective-permute-done((bf16[2,4,256,128]{3,2,1,0:T(8,128)(2,1)S(1)}, bf16[2,4,256,128]{3,2,1,0:T(8,128)(2,1)}, u32[]{:S(2)}, u32[]{:S(2)}) %collective-permute-start) | collective-permute-done | bytes 524320 | tf_op jit(solution)/shard_map/ppermute | solution.py:13
  132.7 14.4 %reshape.197 = bf16[12288,1,4,16]{3,2,1,0:T(4,128)(2,1)} reshape(bf16[16,2,24576]{2,1,0:T(2,128)(2,1)} %copy-done.3) | data formatting | bytes 3145728
  147.1 17.4 %copy.158 = bf16[4,1,16,16,768]{4,2,3,0,1:T(8,128)(2,1)} copy(bf16[4,1,16,16,768]{2,0,4,3,1:T(4,128)(2,1)} %bitcast.206) | data formatting | bytes 3145728 | tf_op jit(solution)/shard_map/all_to_all | solution.py:54
  164.5 3.4 reshape.180
  169.4 14.4 %reshape.203 = bf16[12288,1,4,16]{3,2,1,0:T(4,128)(2,1)} reshape(bf16[16,2,24576]{2,1,0:T(2,128)(2,1)} %all-to-all-done.3) | data formatting | bytes 3145728
  183.8 17.3 %copy.166 = bf16[4,1,16,16,768]{4,2,3,0,1:T(8,128)(2,1)} copy(bf16[4,1,16,16,768]{2,0,4,3,1:T(4,128)(2,1)} %bitcast.207) | data formatting | bytes 3145728 | tf_op jit(solution)/shard_map/all_to_all | solution.py:57
  201.2 3.4 reshape.182
  206.1 142.5 %while.15 = (s32[]{:T(128)}, bf16[4,6,256,128]{2,3,1,0:T(8,128)(2,1)}, f32[4,2,3,256,128]{4,3,2,1,0:T(8,128)}, s32[4]{0:T(128)S(1)}, s32[]{:T(128)}, /*index=5*/...) while((s32[]{:T(128)}, ...), condition=%wide.region_4.5_spmd.clone, body=%wide.region_0.4_spmd.clone.sunk | while | flops 1554380800 | bytes 103924488 | solution.py:99
  213.0 2.0 select_reduce_fusion.2
  216.6 3.0 multiply_reduce_fusion.2
  219.7 2.1 copy-done.1
  221.8 2.3 fusion.65
  225.4 6.1 %fusion.67 = (bf16[768,6,256]{0,2,1:T(8,128)(2,1)}, bf16[768,6,256]{0,2,1:T(8,128)(2,1)}) fusion(f32[6,256,768]{2,1,0:T(8,128)} %copy-done.1, f32[6,256]{1,0:T(8,128)S(1)} %get-tuple-element.456, f32[6,256]{1,0:T(8,128)S(1)} %fusion.64, f32[6,256]{1,0:T(8,128)S(1)} %get-tuple-element.454, f32[6,256,768]{2,1,0:T(8,128)} %copy-done, ...), kind=kLoop, calls=%fused_computation.3.clone.1 | loop fusion | flops 11796480 | bytes 14370816 | tf_op jit(solution)/shard_map/while/body/eval_jaxpr/convert_element_type | solution.py:26
  231.6 2.8 copy.179
  234.4 1.8 convolution_bitcast_fusion.4
  236.2 2.8 copy.180
  239.0 1.8 convolution_bitcast_fusion.5
  248.6 2.0 select_reduce_fusion.2
  252.2 3.0 multiply_reduce_fusion.2
  255.3 2.1 copy-done.1
  257.4 2.3 fusion.65
  261.0 6.1 %fusion.67 = (bf16[768,6,256]{0,2,1:T(8,128)(2,1)}, bf16[768,6,256]{0,2,1:T(8,128)(2,1)}) fusion(f32[6,256,768]{2,1,0:T(8,128)} %copy-done.1, f32[6,256]{1,0:T(8,128)S(1)} %get-tuple-element.456, f32[6,256]{1,0:T(8,128)S(1)} %fusion.64, f32[6,256]{1,0:T(8,128)S(1)} %get-tuple-element.454, f32[6,256,768]{2,1,0:T(8,128)} %copy-done, ...), kind=kLoop, calls=%fused_computation.3.clone.1 | loop fusion | flops 11796480 | bytes 14370816 | tf_op jit(solution)/shard_map/while/body/eval_jaxpr/convert_element_type | solution.py:26
  267.2 2.8 copy.179
  270.0 1.8 convolution_bitcast_fusion.4
  271.8 2.8 copy.180
  274.6 1.8 convolution_bitcast_fusion.5
  284.2 2.0 select_reduce_fusion.2
  287.9 3.0 multiply_reduce_fusion.2
  291.0 2.1 copy-done.1
  293.1 2.3 fusion.65
  296.7 6.1 %fusion.67 = (bf16[768,6,256]{0,2,1:T(8,128)(2,1)}, bf16[768,6,256]{0,2,1:T(8,128)(2,1)}) fusion(f32[6,256,768]{2,1,0:T(8,128)} %copy-done.1, f32[6,256]{1,0:T(8,128)S(1)} %get-tuple-element.456, f32[6,256]{1,0:T(8,128)S(1)} %fusion.64, f32[6,256]{1,0:T(8,128)S(1)} %get-tuple-element.454, f32[6,256,768]{2,1,0:T(8,128)} %copy-done, ...), kind=kLoop, calls=%fused_computation.3.clone.1 | loop fusion | flops 11796480 | bytes 14370816 | tf_op jit(solution)/shard_map/while/body/eval_jaxpr/convert_element_type | solution.py:26
  302.8 2.8 copy.179
  307.4 2.8 copy.180
  310.3 1.8 convolution_bitcast_fusion.5
  319.9 2.0 select_reduce_fusion.2
  323.5 3.0 multiply_reduce_fusion.2
  326.6 2.1 copy-done.1
  328.7 2.3 fusion.65
  332.3 6.1 %fusion.67 = (bf16[768,6,256]{0,2,1:T(8,128)(2,1)}, bf16[768,6,256]{0,2,1:T(8,128)(2,1)}) fusion(f32[6,256,768]{2,1,0:T(8,128)} %copy-done.1, f32[6,256]{1,0:T(8,128)S(1)} %get-tuple-element.456, f32[6,256]{1,0:T(8,128)S(1)} %fusion.64, f32[6,256]{1,0:T(8,128)S(1)} %get-tuple-element.454, f32[6,256,768]{2,1,0:T(8,128)} %copy-done, ...), kind=kLoop, calls=%fused_computation.3.clone.1 | loop fusion | flops 11796480 | bytes 14370816 | tf_op jit(solution)/shard_map/while/body/eval_jaxpr/convert_element_type | solution.py:26
  338.5 2.8 copy.179
  343.1 2.8 copy.180
  345.9 1.8 convolution_bitcast_fusion.5
  348.6 4.1 copy.141
  352.7 2.4 copy.143
  356.4 5.1 %collective-permute-start.2 = (f32[4,2,256,128]{3,0,1,2:T(4,128)S(1)}, f32[4,2,256,128]{3,0,1,2:T(4,128)S(1)}, u32[]{:S(2)}, u32[]{:S(2)}) collective-permute-start(f32[4,2,256,128]{3,0,1,2:T(4,128)S(1)} %fusion.43), channel_id=1, source_target_pairs={{0,15},{1,0},{2,1},{3,2},{4,3},{5,4},{6,5},{7,6},{8,7},{9,8},{10,9... | collective-permute-start | bytes 3145736 | tf_op jit(solution)/shard_map/ppermute | solution.py:13
  361.5 21.4 %collective-permute-done.2 = f32[4,2,256,128]{3,0,1,2:T(4,128)S(1)} collective-permute-done((f32[4,2,256,128]{3,0,1,2:T(4,128)S(1)}, f32[4,2,256,128]{3,0,1,2:T(4,128)S(1)}, u32[]{:S(2)}, u32[]{:S(2)}) %collective-permute-start.2) | collective-permute-done | bytes 1048608 | tf_op jit(solution)/shard_map/ppermute | solution.py:13
  384.6 5.8 %collective-permute-start.3 = (f32[4,2,256,128]{3,0,1,2:T(4,128)}, f32[4,2,256,128]{3,0,1,2:T(4,128)}, u32[]{:S(2)}, u32[]{:S(2)}) collective-permute-start(f32[4,2,256,128]{3,0,1,2:T(4,128)} %fusion.42), channel_id=1, source_target_pairs={{0,15},{1,0},{2,1},{3,2},{4,3},{5,4},{6,5},{7,6},{8,7},{9,8},{10,9... | collective-permute-start | bytes 3145736 | tf_op jit(solution)/shard_map/ppermute | solution.py:13
  390.4 3.8 copy.138
  394.2 6.4 %all-to-all-start.4 = ((bf16[4,1,256,768]{3,0,1,2:T(4,128)(2,1)}), bf16[4,1,256,768]{3,0,1,2:T(4,128)(2,1)}, u32[]{:S(2)}, u32[]{:S(2)}) async-start(bf16[4,1,256,768]{3,0,1,2:T(4,128)(2,1)} %copy.138), calls=%async_computation.4 | async-start | bytes 3145728 | tf_op jit(solution)/shard_map/all_to_all | solution.py:116
  400.6 19.4 %collective-permute-done.3 = f32[4,2,256,128]{3,0,1,2:T(4,128)} collective-permute-done((f32[4,2,256,128]{3,0,1,2:T(4,128)}, f32[4,2,256,128]{3,0,1,2:T(4,128)}, u32[]{:S(2)}, u32[]{:S(2)}) %collective-permute-start.3) | collective-permute-done | bytes 1048608 | tf_op jit(solution)/shard_map/ppermute | solution.py:13
  422.4 16.7 %all_to_all.108 = bf16[4,1,256,128]{3,0,1,2:T(4,128)(2,1)S(1)} all-to-all(bf16[4,1,256,128]{3,0,1,2:T(4,128)(2,1)S(1)} %get-tuple-element.357), channel_id=1, replica_groups=mesh['head'=16,'ctx'=16] {'head'}, dimensions={2} | all-to-all | bytes 524288 | tf_op jit(solution)/shard_map/all_to_all | solution.py:117
  439.2 3.7 all-to-all-start.6
  446.6 3.7 all-to-all-done.6
  (126 shorter events, 56.8 us)
Async XLA Ops:
  0.6 12.0 %copy-start.7 = (bf16[4,1,16,1024]{3,2,1,0:T(8,128)(2,1)S(1)}, bf16[4,1,16,1024]{3,2,1,0:T(8,128)(2,1)}, u32[]{:S(2)}) copy-start(bf16[4,1,16,1024]{3,2,1,0:T(8,128)(2,1)} %param.8) | copy-start | bytes 393220
  5.8 14.2 %all-to-all-start.2 = ((bf16[16,2,4096]{2,1,0:T(2,128)(2,1)}), bf16[16,2,4096]{2,1,0:T(2,128)(2,1)S(1)}, u32[]{:S(2)}, u32[]{:S(2)}) async-start(bf16[16,2,4096]{2,1,0:T(2,128)(2,1)} %reshape.198), calls=%async_computation.2 | async-start | bytes 524288 | tf_op jit(solution)/shard_map/all_to_all | solution.py:56
  20.0 36.5 %all-to-all-start.1 = ((bf16[16,2,4096]{2,1,0:T(2,128)(2,1)}), bf16[16,2,4096]{2,1,0:T(2,128)(2,1)S(1)}, u32[]{:S(2)}, u32[]{:S(2)}) async-start(bf16[16,2,4096]{2,1,0:T(2,128)(2,1)} %reshape.200), calls=%async_computation.1 | async-start | bytes 524288 | tf_op jit(solution)/shard_map/all_to_all | solution.py:55
  38.7 24.3 %copy-start.4 = (bf16[4,1,16,12288]{3,2,1,0:T(8,128)(2,1)S(1)}, bf16[4,1,16,12288]{3,2,1,0:T(8,128)(2,1)}, u32[]{:S(2)}) copy-start(bf16[4,1,16,12288]{3,2,1,0:T(8,128)(2,1)} %param.10) | copy-start | bytes 4718596
  56.5 0.7 copy-start.5
  57.2 35.5 %all-to-all-start = ((bf16[16,2,24576]{2,1,0:T(2,128)(2,1)}), bf16[16,2,24576]{2,1,0:T(2,128)(2,1)S(1)}, u32[]{:S(2)}, u32[]{:S(2)}) async-start(bf16[16,2,24576]{2,1,0:T(2,128)(2,1)} %reshape.196), calls=%async_computation | async-start | bytes 3145728 | tf_op jit(solution)/shard_map/all_to_all | solution.py:54
  92.7 9.6 %copy-start.6 = (bf16[16,2,4096]{2,1,0:T(2,128)(2,1)S(1)}, bf16[16,2,4096]{2,1,0:T(2,128)(2,1)}, u32[]{:S(2)}) copy-start(bf16[16,2,4096]{2,1,0:T(2,128)(2,1)} %copy-done.5) | copy-start | bytes 786436
  92.7 1.2 copy-start.3
  93.9 75.5 %all-to-all-start.3 = ((bf16[16,2,24576]{2,1,0:T(2,128)(2,1)}), bf16[16,2,24576]{2,1,0:T(2,128)(2,1)}, u32[]{:S(2)}, u32[]{:S(2)}) async-start(bf16[16,2,24576]{2,1,0:T(2,128)(2,1)} %reshape.202), calls=%async_computation.3 | async-start | bytes 3145728 | tf_op jit(solution)/shard_map/all_to_all | solution.py:57
  99.7 33.0 %copy-start.8 = (s32[16384]{0:T(1024)S(1)}, s32[16384]{0:T(1024)}, u32[]{:S(2)}) copy-start(s32[16384]{0:T(1024)} %param.11) | copy-start | bytes 196612
  105.0 27.7 %collective-permute-start = (bf16[2,4,256,128]{3,2,1,0:T(8,128)(2,1)S(1)}, bf16[2,4,256,128]{3,2,1,0:T(8,128)(2,1)}, u32[]{:S(2)}, u32[]{:S(2)}) collective-permute-start(bf16[2,4,256,128]{3,2,1,0:T(8,128)(2,1)S(1)} %maximum_bitcast_fusion), channel_id=1, source_target_pairs={{0,1},{1,2},{2,3},{3,4},{4,5},{5,6},{6,7},{7,8},{8,9},{9,10},{10,1... | collective-permute-start | bytes 1572872 | tf_op jit(solution)/shard_map/ppermute | solution.py:13
  132.7 73.4 %collective-permute-start.1 = (bf16[2,4,256,128]{3,2,1,0:T(8,128)(2,1)}, bf16[2,4,256,128]{3,2,1,0:T(8,128)(2,1)}, u32[]{:S(2)}, u32[]{:S(2)}) collective-permute-start(bf16[2,4,256,128]{3,2,1,0:T(8,128)(2,1)} %collective-permute-done), channel_id=1, source_target_pairs={{0,1},{1,2},{2,3},{3,4},{4,5},{5,6},{6,7},{7,8},{8,9},{9,10},{10,1... | collective-permute-start | bytes 1572872 | tf_op jit(solution)/shard_map/ppermute | solution.py:13
  215.0 4.7 %copy-start = (f32[6,256,768]{2,1,0:T(8,128)}, f32[6,256,768]{2,1,0:T(8,128)S(1)}, u32[]{:S(2)}) copy-start(f32[6,256,768]{2,1,0:T(8,128)S(1)} %get-tuple-element.453) | copy-start | bytes 14155780 | tf_op jit(solution)/shard_map/while
  219.7 2.1 copy-start.1
  250.6 4.7 %copy-start = (f32[6,256,768]{2,1,0:T(8,128)}, f32[6,256,768]{2,1,0:T(8,128)S(1)}, u32[]{:S(2)}) copy-start(f32[6,256,768]{2,1,0:T(8,128)S(1)} %get-tuple-element.453) | copy-start | bytes 14155780 | tf_op jit(solution)/shard_map/while
  255.3 2.1 copy-start.1
  286.2 4.7 %copy-start = (f32[6,256,768]{2,1,0:T(8,128)}, f32[6,256,768]{2,1,0:T(8,128)S(1)}, u32[]{:S(2)}) copy-start(f32[6,256,768]{2,1,0:T(8,128)S(1)} %get-tuple-element.453) | copy-start | bytes 14155780 | tf_op jit(solution)/shard_map/while
  290.9 2.1 copy-start.1
  321.9 4.7 %copy-start = (f32[6,256,768]{2,1,0:T(8,128)}, f32[6,256,768]{2,1,0:T(8,128)S(1)}, u32[]{:S(2)}) copy-start(f32[6,256,768]{2,1,0:T(8,128)S(1)} %get-tuple-element.453) | copy-start | bytes 14155780 | tf_op jit(solution)/shard_map/while
  326.6 2.1 copy-start.1
  348.6 4.1 copy-start.2
  356.4 26.5 %collective-permute-start.2 = (f32[4,2,256,128]{3,0,1,2:T(4,128)S(1)}, f32[4,2,256,128]{3,0,1,2:T(4,128)S(1)}, u32[]{:S(2)}, u32[]{:S(2)}) collective-permute-start(f32[4,2,256,128]{3,0,1,2:T(4,128)S(1)} %fusion.43), channel_id=1, source_target_pairs={{0,15},{1,0},{2,1},{3,2},{4,3},{5,4},{6,5},{7,6},{8,7},{9,8},{10,9... | collective-permute-start | bytes 3145736 | tf_op jit(solution)/shard_map/ppermute | solution.py:13
  384.6 35.4 %collective-permute-start.3 = (f32[4,2,256,128]{3,0,1,2:T(4,128)}, f32[4,2,256,128]{3,0,1,2:T(4,128)}, u32[]{:S(2)}, u32[]{:S(2)}) collective-permute-start(f32[4,2,256,128]{3,0,1,2:T(4,128)} %fusion.42), channel_id=1, source_target_pairs={{0,15},{1,0},{2,1},{3,2},{4,3},{5,4},{6,5},{7,6},{8,7},{9,8},{10,9... | collective-permute-start | bytes 3145736 | tf_op jit(solution)/shard_map/ppermute | solution.py:13
  394.2 28.2 %all-to-all-start.4 = ((bf16[4,1,256,768]{3,0,1,2:T(4,128)(2,1)}), bf16[4,1,256,768]{3,0,1,2:T(4,128)(2,1)}, u32[]{:S(2)}, u32[]{:S(2)}) async-start(bf16[4,1,256,768]{3,0,1,2:T(4,128)(2,1)} %copy.138), calls=%async_computation.4 | async-start | bytes 3145728 | tf_op jit(solution)/shard_map/all_to_all | solution.py:116
  439.2 11.2 %all-to-all-start.6 = ((bf16[4,1,256,128]{3,0,1,2:T(4,128)(2,1)}), bf16[4,1,256,128]{3,0,1,2:T(4,128)(2,1)S(1)}, u32[]{:S(2)}, u32[]{:S(2)}) async-start(bf16[4,1,256,128]{3,0,1,2:T(4,128)(2,1)} %get-tuple-element.356), calls=%async_computation.6 | async-start | bytes 524288 | tf_op jit(solution)/shard_map/all_to_all | solution.py:118
where the time goes:
time: 457 us; the launch traced here: 451 us
  local copies, waits for them, and re-layouts  214 us (47%)
  waiting for transfers between devices  73.6 us (16%)
  starting transfers between devices  44.9 us (10%)
  matrix products  43.4 us (9%)
  other arithmetic  41.9 us (9%)
  blocking collectives  16.7 us (4%)
  loops' own time  15.7 us (3%)
    unnamed x26, local copies, waits for them, and re-layouts  105 us
    ppermute x4, waiting for transfers between devices, passed_along(): return lax.ppermute(x, axis, [(i, (i + by) % peers) for i in range(peers)])  66.7 us
    convert_element_type x4, other arithmetic, slot_grads(): dscores = (factor * weights * (dweights - row_dot)).astype(jnp.bfloat16)  24.6 us
    all_to_all x1, local copies, waits for them, and re-layouts, body(): lax.all_to_all(queries, 'head', split_axis=3, concat_axis=2, tiled=True)  17.4 us
    all_to_all x1, local copies, waits for them, and re-layouts, body(): lax.all_to_all(grad_output, 'head', split_axis=3, concat_axis=2, tiled=True)  17.3 us
    all_to_all x1, blocking collectives, body(): lax.all_to_all(key_back, 'head', split_axis=2, concat_axis=3, tiled=True)  16.7 us
    another operation x1, loops' own time, body(): lax.map(visit_slot, (query_all, grad_all, jnp.arange(slot_count, dtype=jn...  15.7 us
    ppermute x4, starting transfers between devices, passed_along(): return lax.ppermute(x, axis, [(i, (i + by) % peers) for i in range(peers)])  12.7 us
  transfers between devices with their start and end apart: 10, of which 5 were waited for; matrix products, arithmetic and copies ran while one was open for 34% of the time, Pallas kernels for 0%

commit v1 on v0

v1 whole, which is shorter than its diff:
```python
import functools
import math

import jax
import jax.numpy as jnp
from jax import lax
from jax.experimental import pallas as pl
from jax.experimental.pallas import tpu as pltpu
from jax.sharding import PartitionSpec as P

MESH = pl.DeviceIdType.MESH
HD = 128
NX = 4
NJ = 8
NCTX = 16
SLOTS = 4
ROWS = 16
GRP = 32
HPG = 12
QW = HPG * HD
NKEY = 17 * GRP
STACK = HPG * GRP
LOG2E = 1.4426950408889634
FACTOR = 1.0 / math.sqrt(HD)
PEERS = tuple((dx, dc) for dx in (2, 1, 3, 0) for dc in (0, 1) if (dx, dc) != (0, 0))


def kernel(
    q_ref, k_ref, v_ref, g_ref, doc_ref, dq_ref, dk_ref, dv_ref,
    qr, gr, dqs, kv, qc, gc, kc, vc, bias, start, acc, dks, dko, rx, home,
    q_ss, q_rs, a_ss, a_rs, f_ss, f_rs, dq_ss, dq_rs, dk_ss, dk_rs, h_ss, h_rs,
):
    head = lax.axis_index("head")
    c = lax.axis_index("ctx")
    x, y, core = head // 4, (head // 2) % 2, head % 2
    me = x * 2 + core
    other = 1 - y

    def dev(nj, ny, nc):
        return dict(head=(nj // 2) * 4 + ny * 2 + nj % 2, ctx=nc)

    def hop(by):
        return (c + by + NCTX) % NCTX

    def peer(dx, dc):
        return ((x + dx) % NX) * 2 + (core + dc) % 2

    def remote(src, dst, ss, rs, to):
        return pltpu.make_async_remote_copy(
            src_ref=src, dst_ref=dst, send_sem=ss, recv_sem=rs, device_id=to, device_id_type=MESH
        )

    def arrived(ref, sem):
        pltpu.make_async_copy(ref, ref, sem).wait()

    barrier = pltpu.get_barrier_semaphore()
    partners = [dev(peer(*p), y, c) for p in PEERS] + [dev(me, other, c)]
    partners += [dev(me, ny, hop(b)) for b in (1, 2, -1, -2) for ny in (y, other)]
    for to in partners:
        pl.semaphore_signal(barrier, inc=1, device_id=to, device_id_type=MESH)
    pl.semaphore_wait(barrier, len(partners))

    def kv_src(ref, j):
        return ref.at[:, 0, :, pl.ds(pl.multiple_of(j * HD, HD), HD)]

    def kv_dst(n, j):
        return kv.at[n, :, 2, j // 2, y, pl.ds(pl.multiple_of((j % 2) * ROWS, ROWS), ROWS)]

    for p in PEERS:
        j = peer(*p)
        for n, ref in enumerate((k_ref, v_ref)):
            remote(kv_src(ref, j), kv_dst(n, me), a_ss.at[n, j], a_rs.at[n, me], dev(j, y, c)).start()
    for n, ref in enumerate((k_ref, v_ref)):
        pltpu.make_async_copy(kv_src(ref, me), kv_dst(n, me), a_rs.at[n, me]).start()

    def q_src(ref, a, j):
        return ref.at[a, 0, :, pl.ds(pl.multiple_of(j * QW, QW), QW)]

    def send_q(a):
        for p in PEERS:
            j = peer(*p)
            for n, (ref, to) in enumerate(((q_ref, qr), (g_ref, gr))):
                remote(q_src(ref, a, j), to.at[a, me], q_ss.at[n, a, j], q_rs.at[n, a, me], dev(j, y, c)).start()
        for n, (ref, to) in enumerate(((q_ref, qr), (g_ref, gr))):
            pltpu.make_async_copy(q_src(ref, a, me), to.at[a, me], q_rs.at[n, a, me]).start()

    send_q(0)

    doc = doc_ref[...]
    row = lax.broadcasted_iota(jnp.int32, doc.shape, 0)
    lane = lax.broadcasted_iota(jnp.int32, doc.shape, 1)
    before = pltpu.roll(doc, 1, 1)
    before = jnp.where(lane == 0, pltpu.roll(before, 1, 0), before)
    run = jnp.where(doc != before, row * HD + lane, 0)
    for s in (1, 2, 4, 8, 16, 32, 64):
        run = jnp.maximum(run, jnp.where(lane >= s, pltpu.roll(run, s, 1), 0))
    last = jnp.broadcast_to(jnp.max(run, axis=1, keepdims=True), doc.shape)
    carry = jnp.where(row >= 1, pltpu.roll(last, 1, 0), 0)
    for s in (1, 2, 4, 8, 16, 32, 64):
        carry = jnp.maximum(carry, jnp.where(row >= s, pltpu.roll(carry, s, 0), 0))
    start[...] = jnp.maximum(run, carry)

    for n in range(2):
        for j in range(NJ):
            arrived(kv_dst(n, j), a_rs.at[n, j])
    onward = (
        (2, dev(me, other, c), 0),
        (1, dev(me, y, hop(1)), (c + 1) // NCTX),
        (1, dev(me, other, hop(1)), (c + 1) // NCTX),
        (0, dev(me, y, hop(2)), (c + 2) // NCTX),
        (0, dev(me, other, hop(2)), (c + 2) // NCTX),
    )

    def onward_copy(n, a):
        piece, to, ahead = onward[n]
        at = (a + ahead) % SLOTS
        return remote(kv.at[:, a, 2, :, y], kv.at[:, at, piece, :, y], f_ss.at[a, n], f_rs.at[at, n], to)

    def onward_slot(a, _):
        for n in range(5):
            onward_copy(n, a).start()
        return _

    lax.fori_loop(0, SLOTS, onward_slot, 0)

    def send_rest(a, _):
        send_q(a)
        return _

    lax.fori_loop(1, SLOTS, send_rest, 0)

    key_at = lax.broadcasted_iota(jnp.int32, (NKEY, HD), 0)
    lane8 = lax.broadcasted_iota(jnp.int32, (8, HD), 1)
    row_in = lane8 % GRP

    def dq_dst(a, j):
        return dq_ref.at[a, 0, :, pl.ds(pl.multiple_of(j * QW, QW), QW)]

    def chunk(a, i):
        xs = (x + i + (i // 2) * (1 - 2 * (i % 2))) % NX
        for nc in range(2):
            for n, to in enumerate((qr, gr)):
                arrived(to.at[a, 2 * xs + nc], q_rs.at[n, a, 2 * xs + nc])
        off = 2 * xs + y
        for h in range(HPG):
            at = pl.ds(h * HD, HD)
            qc[pl.ds(h * GRP, GRP), :] = qr[a, pl.ds(2 * xs, 2), :, at].reshape(GRP, HD)
            gc[pl.ds(h * GRP, GRP), :] = gr[a, pl.ds(2 * xs, 2), :, at].reshape(GRP, HD)
        for t in range(17):
            at = off + t
            kc[pl.ds(t * GRP, GRP), :] = kv[0, a, at // 8, (at % 8) // 2, at % 2]
            vc[pl.ds(t * GRP, GRP), :] = kv[1, a, at // 8, (at % 8) // 2, at % 2]
        first = (a * NCTX + c) * 256 + off * GRP
        line = jnp.broadcast_to(start[pl.ds((a * NCTX + c) * 2 + off // 4, 1), :], (8, HD))
        line = pltpu.roll(line, (HD - GRP * (off % 4)) % HD, 1)
        line = jnp.where(lane8 < GRP, line, 0)
        line = line + pltpu.roll(line, GRP, 1)
        line = line + pltpu.roll(line, 2 * GRP, 1)
        low = jnp.maximum(line - (first - 512), row_in + 1)[:1]
        high = (row_in + 512)[:1]
        bias[...] = jnp.where((key_at >= low) & (key_at <= high), 0.0, -1e30)
        nt = (((1,), (1,)), ((), ()))
        scores = lax.dot_general(kc[...], qc[...], nt, preferred_element_type=jnp.float32)
        dweights = lax.dot_general(vc[...], gc[...], nt, preferred_element_type=jnp.float32)
        both = jnp.concatenate([bias[...]] * (STACK // HD), axis=1)
        scaled = scores * (FACTOR * LOG2E) + both
        top = jnp.max(scaled, axis=0, keepdims=True)
        exponent = jnp.exp2(scaled - top)
        total = jnp.sum(exponent, axis=0, keepdims=True)
        cross = jnp.sum(exponent * dweights, axis=0, keepdims=True)
        inverse = 1.0 / total
        weights = exponent * inverse
        dscores = (weights * (dweights - cross * inverse)).astype(jnp.bfloat16)
        weights = weights.astype(jnp.bfloat16)
        nn = (((1,), (0,)), ((), ()))
        dv = lax.dot_general(weights, gc[...], nn, preferred_element_type=jnp.float32)
        dk = lax.dot_general(dscores, qc[...], nn, preferred_element_type=jnp.float32)
        tn = (((0,), (0,)), ((), ()))
        dq = lax.dot_general(dscores, kc[...], tn, preferred_element_type=jnp.float32)
        acc[0, pl.ds(off, 17)] += dk.reshape(17, GRP, HD)
        acc[1, pl.ds(off, 17)] += dv.reshape(17, GRP, HD)
        dq = (dq * FACTOR).astype(jnp.bfloat16)
        for h in range(HPG):
            dqs[a, pl.ds(2 * xs, 2), :, pl.ds(h * HD, HD)] = dq[h * GRP : (h + 1) * GRP].reshape(2, ROWS, HD)
        for nc in range(2):
            j = 2 * xs + nc

            @pl.when(j == me)
            def _():
                pltpu.make_async_copy(dqs.at[a, j], dq_dst(a, me), dq_rs.at[a, me]).start()

            @pl.when(j != me)
            def _():
                remote(dqs.at[a, j], dq_dst(a, me), dq_ss.at[a, j], dq_rs.at[a, me], dev(j, y, c)).start()

    near, far = 1 - (c + 15) // NCTX, 1 - (c + 14) // NCTX
    back = (
        (2, other, dev(me, other, c), 0),
        (1, y, dev(me, y, hop(-1)), near),
        (1, other, dev(me, other, hop(-1)), near),
        (0, y, dev(me, y, hop(-2)), far),
        (0, other, dev(me, other, hop(-2)), far),
    )

    def back_copy(n, a):
        piece, half, to, behind = back[n]
        at = (a + SLOTS - behind) % SLOTS
        return remote(dks.at[a, :, piece, :, half], rx.at[at, n], dk_ss.at[a, n], dk_rs.at[at, n], to)

    def slot(a, _):
        for n in range(5):
            arrived(rx.at[a, n], f_rs.at[a, n])
        acc[...] = jnp.zeros_like(acc)

        def one(i, _):
            chunk(a, i)
            return _

        lax.fori_loop(0, NX, one, 0)
        dks[a, 0] = (acc[0] * FACTOR).astype(jnp.bfloat16).reshape(3, NX, 2, GRP, HD)
        dks[a, 1] = acc[1].astype(jnp.bfloat16).reshape(3, NX, 2, GRP, HD)
        for xx in range(NX):
            dko[a, 0, xx] = acc[0, 16 + 2 * xx + y] * FACTOR
            dko[a, 1, xx] = acc[1, 16 + 2 * xx + y]
        for n in range(5):
            back_copy(n, a).start()
        return _

    lax.fori_loop(0, SLOTS, slot, 0)

    def reduce(a, _):
        for n in range(5):
            arrived(rx.at[a, n], dk_rs.at[a, n])
        total = dko[a]
        for n in range(5):
            total = total + rx[a, n].astype(jnp.float32)
        home[:, a] = total.astype(jnp.bfloat16)
        return _

    lax.fori_loop(0, SLOTS, reduce, 0)

    def home_src(n, j):
        return home.at[n, :, j // 2, pl.ds(pl.multiple_of((j % 2) * ROWS, ROWS), ROWS)]

    def home_dst(n, j):
        return (dk_ref, dv_ref)[n].at[:, 0, :, pl.ds(pl.multiple_of(j * HD, HD), HD)]

    for n in range(2):
        pltpu.make_async_copy(home_src(n, me), home_dst(n, me), h_rs.at[n, me]).start()
        for p in PEERS:
            j = peer(*p)
            remote(home_src(n, j), home_dst(n, me), h_ss.at[n, j], h_rs.at[n, me], dev(j, y, c)).start()

    def drain(a, _):
        for j in range(NJ):
            arrived(dqs.at[a, j], dq_rs.at[a, j])
        for p in PEERS:
            j = peer(*p)
            for n, to in enumerate((qr, gr)):
                arrived(to.at[a, j], q_ss.at[n, a, j])
            arrived(dqs.at[a, j], dq_ss.at[a, j])
        for n in range(5):
            arrived(rx.at[a, n], f_ss.at[a, n])
            arrived(rx.at[a, n], dk_ss.at[a, n])
        return _

    lax.fori_loop(0, SLOTS, drain, 0)
    for n in range(2):
        for p in PEERS:
            j = peer(*p)
            arrived(kv_dst(n, j), a_ss.at[n, j])
            arrived(kv_dst(n, j), h_ss.at[n, j])
        for j in range(NJ):
            arrived(kv_dst(n, j), h_rs.at[n, j])


def body(queries, key_vectors, value_vectors, grad_output, doc_ids):
    bf, f32, dma = jnp.bfloat16, jnp.float32, pltpu.SemaphoreType.DMA
    hbm = pl.BlockSpec(memory_space=pl.ANY)
    vmem = pltpu.VMEM
    like = jax.ShapeDtypeStruct
    return pl.pallas_call(
        kernel,
        out_shape=(
            like(queries.shape, bf),
            like(key_vectors.shape, bf),
            like(value_vectors.shape, bf),
        ),
        in_specs=[hbm] * 4 + [pl.BlockSpec(memory_space=vmem)],
        out_specs=(hbm,) * 3,
        scratch_shapes=[
            vmem((SLOTS, NJ, ROWS, QW), bf),
            vmem((SLOTS, NJ, ROWS, QW), bf),
            vmem((SLOTS, NJ, ROWS, QW), bf),
            vmem((2, SLOTS, 3, NX, 2, GRP, HD), bf),
            vmem((STACK, HD), bf),
            vmem((STACK, HD), bf),
            vmem((NKEY, HD), bf),
            vmem((NKEY, HD), bf),
            vmem((NKEY, HD), f32),
            vmem((HD, HD), jnp.int32),
            vmem((2, 24, GRP, HD), f32),
            vmem((SLOTS, 2, 3, NX, 2, GRP, HD), bf),
            vmem((SLOTS, 2, NX, GRP, HD), f32),
            vmem((SLOTS, 5, 2, NX, GRP, HD), bf),
            vmem((2, SLOTS, NX, GRP, HD), bf),
            dma((2, SLOTS, NJ)),
            dma((2, SLOTS, NJ)),
            dma((2, NJ)),
            dma((2, NJ)),
            dma((SLOTS, 5)),
            dma((SLOTS, 5)),
            dma((SLOTS, NJ)),
            dma((SLOTS, NJ)),
            dma((SLOTS, 5)),
            dma((SLOTS, 5)),
            dma((2, NJ)),
            dma((2, NJ)),
        ],
        compiler_params=pltpu.CompilerParams(
            collective_id=0, has_side_effects=True, vmem_limit_bytes=48 << 20
        ),
    )(queries, key_vectors, value_vectors, grad_output, doc_ids.reshape(HD, HD))


def solution(mesh):
    placed = P(None, "ctx", "head", None)
    return jax.shard_map(
        body,
        mesh=mesh,
        in_specs=(placed,) * 4 + (P(),),
        out_specs=(placed,) * 3,
        check_vma=False,
    )
```

time: 457 us -> 106 us (0.23)
  the two profiles are of different devices: /device:TPU:1 before, /device:TPU:217 now
where the time goes in v1:
time: 106 us
  Pallas kernels  97.4 us (92%)
  local copies, waits for them, and re-layouts  7.91 us (7%)
    pallas_call x1, Pallas kernels, body(): pl.pallas_call(kernel, out_shape=(like(queries.shape, bf), like(key_vecto...  97.4 us
    unnamed x13, local copies, waits for them, and re-layouts  7.91 us

profile of v1, /device:TPU:217, one launch (start us, length us, event | category | flops | bytes accessed | tf_op | source)
XLA Modules:
  0.0 105.9 jit_solution(13878180241510718271)
XLA Ops:
  0.6 0.0 copy-start
  0.6 1.4 %copy-done = bf16[4,1,16,12288]{3,2,1,0:T(8,128)(2,1)S(1)} copy-done((bf16[4,1,16,12288]{3,2,1,0:T(8,128)(2,1)S(1)}, bf16[4,1,16,12288]{3,2,1,0:T(8,128)(2,1)}, u32[]{:S(2)}) %copy-start) | copy-done | bytes 1572888
  2.0 0.0 copy-start.1
  2.0 1.4 %copy-done.1 = bf16[4,1,16,12288]{3,2,1,0:T(8,128)(2,1)S(1)} copy-done((bf16[4,1,16,12288]{3,2,1,0:T(8,128)(2,1)S(1)}, bf16[4,1,16,12288]{3,2,1,0:T(8,128)(2,1)}, u32[]{:S(2)}) %copy-start.1) | copy-done | bytes 1572888
  3.4 0.0 copy-start.2
  3.5 0.9 copy-done.2
  4.4 0.0 copy-start.3
  4.4 0.9 copy-done.3
  5.3 0.0 copy-start.4
  5.3 0.8 copy-done.4
  6.1 97.4 %shard_map.76 = (bf16[4,1,16,12288]{3,2,1,0:T(8,128)(2,1)S(1)}, bf16[4,1,16,1024]{3,2,1,0:T(8,128)(2,1)S(1)}, bf16[4,1,16,1024]{3,2,1,0:T(8,128)(2,1)S(1)}) custom-call(bf16[4,1,16,12288]{3,2,1,0:T(8,128)(2,1)S(1)} %copy-done, bf16[4,1,16,1024]{3,2,1,0:T(8,128)(2,1)S(1)} %copy-done.2, bf16[4,1,16,1024]{3,2,1,0:T(8,128)(2,1)S(1)} %copy-done.3, ...), custom_call_target="tpu_custom_call" | custom-call | tf_op jit(solution)/shard_map/pallas_call | solution.py:282
  103.5 1.1 %copy.11 = bf16[4,1,16,12288]{3,2,1,0:T(8,128)(2,1)} copy(bf16[4,1,16,12288]{3,2,1,0:T(8,128)(2,1)S(1)} %get-tuple-element.6) | data formatting | bytes 3145728
  104.6 0.7 copy.12
  105.3 0.7 copy.13
Async XLA Ops:
  0.6 1.4 %copy-start = (bf16[4,1,16,12288]{3,2,1,0:T(8,128)(2,1)S(1)}, bf16[4,1,16,12288]{3,2,1,0:T(8,128)(2,1)}, u32[]{:S(2)}) copy-start(bf16[4,1,16,12288]{3,2,1,0:T(8,128)(2,1)} %q_ref.1) | copy-start | bytes 4718596
  2.0 1.4 %copy-start.1 = (bf16[4,1,16,12288]{3,2,1,0:T(8,128)(2,1)S(1)}, bf16[4,1,16,12288]{3,2,1,0:T(8,128)(2,1)}, u32[]{:S(2)}) copy-start(bf16[4,1,16,12288]{3,2,1,0:T(8,128)(2,1)} %g_ref.1) | copy-start | bytes 4718596
  3.4 0.9 copy-start.2
  4.4 0.9 copy-start.3
  5.3 0.8 copy-start.4

commit v2 on v1

--- a/solution.py
+++ b/solution.py
@@ -13,6 +13,7 @@
 NX = 4
 NJ = 8
 NCTX = 16
+NZ = 8
 SLOTS = 4
 ROWS = 16
 GRP = 32
@@ -27,7 +28,7 @@
 
 def kernel(
     q_ref, k_ref, v_ref, g_ref, doc_ref, dq_ref, dk_ref, dv_ref,
-    qr, gr, dqs, kv, qc, gc, kc, vc, bias, start, acc, dks, dko, rx, home,
+    qr, gr, dqs, kv, qc, gc, kc, vc, bias, start, acc, dks, dko, rx, dsum, own, home,
     q_ss, q_rs, a_ss, a_rs, f_ss, f_rs, dq_ss, dq_rs, dk_ss, dk_rs, h_ss, h_rs,
 ):
     head = lax.axis_index("head")
@@ -103,31 +104,55 @@
     for n in range(2):
         for j in range(NJ):
             arrived(kv_dst(n, j), a_rs.at[n, j])
-    onward = (
-        (2, dev(me, other, c), 0),
-        (1, dev(me, y, hop(1)), (c + 1) // NCTX),
-        (1, dev(me, other, hop(1)), (c + 1) // NCTX),
-        (0, dev(me, y, hop(2)), (c + 2) // NCTX),
-        (0, dev(me, other, hop(2)), (c + 2) // NCTX),
-    )
-
-    def onward_copy(n, a):
-        piece, to, ahead = onward[n]
-        at = (a + ahead) % SLOTS
-        return remote(kv.at[:, a, 2, :, y], kv.at[:, at, piece, :, y], f_ss.at[a, n], f_rs.at[at, n], to)
-
-    def onward_slot(a, _):
-        for n in range(5):
-            onward_copy(n, a).start()
-        return _
-
-    lax.fori_loop(0, SLOTS, onward_slot, 0)
+    z = c % NZ
+    over, step = dev(me, other, c), (c + 1) // NCTX
+    after = dev(me, (y + (z + 1) // NZ) % 2, hop(1))
+    halves = ((y + 1 - (z + NZ - 2) // NZ) % 2, (y + 1 - (z + NZ - 1) // NZ) % 2, y)
+
+    def half(a, piece, of):
+        return kv.at[:, a, piece, :, halves[of]]
+
+    def own_out(a):
+        at = (a + step) % SLOTS
+        return (
+            remote(half(a, 2, 2), half(a, 2, 2), f_ss.at[a, 0], f_rs.at[a, 0], over),
+            remote(half(a, 2, 2), half(at, 1, 2), f_ss.at[a, 1], f_rs.at[at, 1], after),
+        )
+
+    def near_out(a):
+        at = (a + step) % SLOTS
+        return (
+            remote(half(a, 1, 1), half(at, 0, 1), f_ss.at[a, 3], f_rs.at[at, 3], after),
+            remote(half(a, 1, 1), half(a, 1, 1), f_ss.at[a, 2], f_rs.at[a, 2], over),
+        )
+
+    def far_out(a):
+        return (remote(half(a, 0, 0), half(a, 0, 0), f_ss.at[a, 4], f_rs.at[a, 4], over),)
+
+    def onward(copies, a, came=None):
+        if came is not None:
+            arrived(rx.at[a, 0], f_rs.at[a, came])
+        for copy in copies(a):
+            copy.start()
+
+    def own_slot(a, _):
+        onward(own_out, a)
+        return _
+
+    lax.fori_loop(0, SLOTS, own_slot, 0)
 
     def send_rest(a, _):
         send_q(a)
         return _
 
     lax.fori_loop(1, SLOTS, send_rest, 0)
+
+    def near_slot(a, _):
+        onward(near_out, a, 1)
+        return _
+
+    lax.fori_loop(0, SLOTS, near_slot, 0)
+    onward(far_out, 0, 3)
 
     key_at = lax.broadcasted_iota(jnp.int32, (NKEY, HD), 0)
     lane8 = lax.broadcasted_iota(jnp.int32, (8, HD), 1)
@@ -137,7 +162,7 @@
         return dq_ref.at[a, 0, :, pl.ds(pl.multiple_of(j * QW, QW), QW)]
 
     def chunk(a, i):
-        xs = (x + i + (i // 2) * (1 - 2 * (i % 2))) % NX
+        xs = (x + 2 * (i % 2) + i // 2) % NX
         for nc in range(2):
             for n, to in enumerate((qr, gr)):
                 arrived(to.at[a, 2 * xs + nc], q_rs.at[n, a, 2 * xs + nc])
@@ -193,63 +218,81 @@
             def _():
                 remote(dqs.at[a, j], dq_dst(a, me), dq_ss.at[a, j], dq_rs.at[a, me], dev(j, y, c)).start()
 
-    near, far = 1 - (c + 15) // NCTX, 1 - (c + 14) // NCTX
-    back = (
-        (2, other, dev(me, other, c), 0),
-        (1, y, dev(me, y, hop(-1)), near),
-        (1, other, dev(me, other, hop(-1)), near),
-        (0, y, dev(me, y, hop(-2)), far),
-        (0, other, dev(me, other, hop(-2)), far),
-    )
-
-    def back_copy(n, a):
-        piece, half, to, behind = back[n]
-        at = (a + SLOTS - behind) % SLOTS
-        return remote(dks.at[a, :, piece, :, half], rx.at[at, n], dk_ss.at[a, n], dk_rs.at[at, n], to)
-
-    def slot(a, _):
-        for n in range(5):
-            arrived(rx.at[a, n], f_rs.at[a, n])
+    def swap_copy(a, piece):
+        return remote(dks.at[a, piece], rx.at[a, piece], dk_ss.at[a, piece], dk_rs.at[a, piece], over)
+
+    def swap(a):
+        for piece in range(3):
+            for n, scale in enumerate((FACTOR, 1.0)):
+                for xx in range(NX):
+                    at = piece * 8 + 2 * xx
+                    dko[a, piece, n, xx] = acc[n, at + halves[piece]] * scale
+                    dks[a, piece, n, xx] = (acc[n, at + 1 - halves[piece]] * scale).astype(jnp.bfloat16)
+            swap_copy(a, piece).start()
+
+    def owner_copy(a, piece):
+        hops = 2 - piece
+        at = (a + SLOTS - 1 + (c + NCTX - hops) // NCTX) % SLOTS
+        to = dev(me, halves[piece], hop(-hops))
+        return remote(dsum.at[a, piece], own.at[at, piece], dk_ss.at[a, 3 + piece], dk_rs.at[at, 3 + piece], to)
+
+    def pass_back(a):
+        for piece in range(2):
+            arrived(rx.at[a, piece], dk_rs.at[a, piece])
+            dsum[a, piece] = (dko[a, piece] + rx[a, piece].astype(jnp.float32)).astype(jnp.bfloat16)
+            owner_copy(a, piece).start()
+
+    def slot(a, carry):
+        @pl.when(a < SLOTS - 1)
+        def _():
+            onward(far_out, a + 1, 3)
+
+        for n in (0, 2, 4):
+            arrived(rx.at[a, 0], f_rs.at[a, n])
         acc[...] = jnp.zeros_like(acc)
 
-        def one(i, _):
+        def one(i, carry):
             chunk(a, i)
-            return _
+
+            @pl.when((i == 1) & (a > 0))
+            def _():
+                pass_back(a - 1)
+
+            return carry
 
         lax.fori_loop(0, NX, one, 0)
-        dks[a, 0] = (acc[0] * FACTOR).astype(jnp.bfloat16).reshape(3, NX, 2, GRP, HD)
-        dks[a, 1] = acc[1].astype(jnp.bfloat16).reshape(3, NX, 2, GRP, HD)
-        for xx in range(NX):
-            dko[a, 0, xx] = acc[0, 16 + 2 * xx + y] * FACTOR
-            dko[a, 1, xx] = acc[1, 16 + 2 * xx + y]
-        for n in range(5):
-            back_copy(n, a).start()
-        return _
+        swap(a)
+        return carry
 
     lax.fori_loop(0, SLOTS, slot, 0)
 
+    pass_back(SLOTS - 1)
+
     def reduce(a, _):
-        for n in range(5):
-            arrived(rx.at[a, n], dk_rs.at[a, n])
-        total = dko[a]
-        for n in range(5):
-            total = total + rx[a, n].astype(jnp.float32)
+        for n in (2, 3, 4):
+            arrived(rx.at[a, 0], dk_rs.at[a, n])
+        total = dko[a, 2] + rx[a, 2].astype(jnp.float32)
+        for n in range(2):
+            total = total + own[a, n].astype(jnp.float32)
         home[:, a] = total.astype(jnp.bfloat16)
         return _
 
-    lax.fori_loop(0, SLOTS, reduce, 0)
-
-    def home_src(n, j):
-        return home.at[n, :, j // 2, pl.ds(pl.multiple_of((j % 2) * ROWS, ROWS), ROWS)]
-
-    def home_dst(n, j):
-        return (dk_ref, dv_ref)[n].at[:, 0, :, pl.ds(pl.multiple_of(j * HD, HD), HD)]
-
-    for n in range(2):
-        pltpu.make_async_copy(home_src(n, me), home_dst(n, me), h_rs.at[n, me]).start()
-        for p in PEERS:
-            j = peer(*p)
-            remote(home_src(n, j), home_dst(n, me), h_ss.at[n, j], h_rs.at[n, me], dev(j, y, c)).start()
+    def home_src(n, j, at):
+        return home.at[n, at, j // 2, pl.ds(pl.multiple_of((j % 2) * ROWS, ROWS), ROWS)]
+
+    def home_dst(n, j, at):
+        return (dk_ref, dv_ref)[n].at[at, 0, :, pl.ds(pl.multiple_of(j * HD, HD), HD)]
+
+    for part, (low, many) in enumerate(((0, SLOTS - 1), (SLOTS - 1, 1))):
+        lax.fori_loop(low, low + many, reduce, 0)
+        at = pl.ds(low, many)
+        for n in range(2):
+            pltpu.make_async_copy(home_src(n, me, at), home_dst(n, me, at), h_rs.at[part, n, me]).start()
+            for p in PEERS:
+                j = peer(*p)
+                remote(
+                    home_src(n, j, at), home_dst(n, me, at), h_ss.at[part, n, j], h_rs.at[part, n, me], dev(j, y, c)
+                ).start()
 
     def drain(a, _):
         for j in range(NJ):
@@ -260,8 +303,8 @@
                 arrived(to.at[a, j], q_ss.at[n, a, j])
             arrived(dqs.at[a, j], dq_ss.at[a, j])
         for n in range(5):
-            arrived(rx.at[a, n], f_ss.at[a, n])
-            arrived(rx.at[a, n], dk_ss.at[a, n])
+            arrived(rx.at[a, 0], f_ss.at[a, n])
+            arrived(rx.at[a, 0], dk_ss.at[a, n])
         return _
 
     lax.fori_loop(0, SLOTS, drain, 0)
@@ -269,14 +312,16 @@
         for p in PEERS:
             j = peer(*p)
             arrived(kv_dst(n, j), a_ss.at[n, j])
-            arrived(kv_dst(n, j), h_ss.at[n, j])
-        for j in range(NJ):
-            arrived(kv_dst(n, j), h_rs.at[n, j])
+        for part, at in enumerate((pl.ds(0, SLOTS - 1), pl.ds(SLOTS - 1, 1))):
+            for p in PEERS:
+                arrived(home_src(n, 0, at), h_ss.at[part, n, peer(*p)])
+            for j in range(NJ):
+                arrived(home_src(n, 0, at), h_rs.at[part, n, j])
 
 
 def body(queries, key_vectors, value_vectors, grad_output, doc_ids):
     bf, f32, dma = jnp.bfloat16, jnp.float32, pltpu.SemaphoreType.DMA
-    hbm = pl.BlockSpec(memory_space=pl.ANY)
+    hbm = pl.BlockSpec(memory_space=pltpu.HBM)
     vmem = pltpu.VMEM
     like = jax.ShapeDtypeStruct
     return pl.pallas_call(
@@ -300,9 +345,11 @@
             vmem((NKEY, HD), f32),
             vmem((HD, HD), jnp.int32),
             vmem((2, 24, GRP, HD), f32),
-            vmem((SLOTS, 2, 3, NX, 2, GRP, HD), bf),
-            vmem((SLOTS, 2, NX, GRP, HD), f32),
-            vmem((SLOTS, 5, 2, NX, GRP, HD), bf),
+            vmem((SLOTS, 3, 2, NX, GRP, HD), bf),
+            vmem((SLOTS, 3, 2, NX, GRP, HD), f32),
+            vmem((SLOTS, 3, 2, NX, GRP, HD), bf),
+            vmem((SLOTS, 2, 2, NX, GRP, HD), bf),
+            vmem((SLOTS, 2, 2, NX, GRP, HD), bf),
             vmem((2, SLOTS, NX, GRP, HD), bf),
             dma((2, SLOTS, NJ)),
             dma((2, SLOTS, NJ)),
@@ -314,11 +361,11 @@
             dma((SLOTS, NJ)),
             dma((SLOTS, 5)),
             dma((SLOTS, 5)),
-            dma((2, NJ)),
-            dma((2, NJ)),
+            dma((2, 2, NJ)),
+            dma((2, 2, NJ)),
         ],
         compiler_params=pltpu.CompilerParams(
-            collective_id=0, has_side_effects=True, vmem_limit_bytes=48 << 20
+            collective_id=0, has_side_effects=True, vmem_limit_bytes=62 << 20
         ),
     )(queries, key_vectors, value_vectors, grad_output, doc_ids.reshape(HD, HD))
 

time: 106 us -> 79.1 us (0.75)
  the two profiles are of different devices: /device:TPU:217 before, /device:TPU:1 now
where the time goes in v2:
time: 79.1 us; the launch traced here: 78.9 us
  Pallas kernels  74.2 us (94%)
  local copies, waits for them, and re-layouts  4.01 us (5%)
    pallas_call x1, Pallas kernels, body(): pl.pallas_call(kernel, out_shape=(like(queries.shape, bf), like(key_vecto...  74.2 us
    unnamed x7, local copies, waits for them, and re-layouts  4.01 us

profile of v2, /device:TPU:1, one launch (start us, length us, event | category | flops | bytes accessed | tf_op | source)
XLA Modules:
  0.0 78.9 jit_solution(16973280656133838883)
XLA Ops:
  0.6 74.2 %shard_map.76 = (bf16[4,1,16,12288]{3,2,1,0:T(8,128)(2,1)}, bf16[4,1,16,1024]{3,2,1,0:T(8,128)(2,1)}, bf16[4,1,16,1024]{3,2,1,0:T(8,128)(2,1)}) custom-call(bf16[4,1,16,12288]{3,2,1,0:T(8,128)(2,1)} %q_ref.1, bf16[4,1,16,1024]{3,2,1,0:T(8,128)(2,1)} %k_ref.1, bf16[4,1,16,1024]{3,2,1,0:T(8,128)(2,1)} %v_ref.1, bf16[4,1,16,12288]{3,2,1,0:T(8,128)(2,1)} %g_ref.1, ...), custom_call_target="tpu_custom_call" | custom-call | tf_op jit(solution)/shard_map/pallas_call | solution.py:327
  74.9 0.0 copy-start.1
  74.9 0.0 copy-start
  74.9 2.7 %copy.11 = bf16[4,1,16,12288]{3,2,1,0:T(8,128)(2,1)} copy(bf16[4,1,16,12288]{3,2,1,0:T(8,128)(2,1)} %get-tuple-element.6) | data formatting | bytes 3145728
  77.6 0.0 copy-done.1
  77.6 0.7 copy.12
  78.3 0.0 copy-done
  78.3 0.7 copy.13
Async XLA Ops:
  74.9 2.7 %copy-start.1 = (bf16[4,1,16,1024]{3,2,1,0:T(8,128)(2,1)S(1)}, bf16[4,1,16,1024]{3,2,1,0:T(8,128)(2,1)}, u32[]{:S(2)}) copy-start(bf16[4,1,16,1024]{3,2,1,0:T(8,128)(2,1)} %get-tuple-element.7) | copy-start | bytes 393220
  74.9 3.4 %copy-start = (bf16[4,1,16,1024]{3,2,1,0:T(8,128)(2,1)S(1)}, bf16[4,1,16,1024]{3,2,1,0:T(8,128)(2,1)}, u32[]{:S(2)}) copy-start(bf16[4,1,16,1024]{3,2,1,0:T(8,128)(2,1)} %get-tuple-element.8) | copy-start | bytes 393220

commit v3 on v2

--- a/solution.py
+++ b/solution.py
@@ -29,7 +29,7 @@
 def kernel(
     q_ref, k_ref, v_ref, g_ref, doc_ref, dq_ref, dk_ref, dv_ref,
     qr, gr, dqs, kv, qc, gc, kc, vc, bias, start, acc, dks, dko, rx, dsum, own, home,
-    q_ss, q_rs, a_ss, a_rs, f_ss, f_rs, dq_ss, dq_rs, dk_ss, dk_rs, h_ss, h_rs,
+    q_ss, q_rs, a_ss, a_rs, f_ss, f_rs, dq_ss, dq_rs, dk_ss, dk_rs, h_ss, h_rs, met,
 ):
     head = lax.axis_index("head")
     c = lax.axis_index("ctx")
@@ -54,12 +54,36 @@
     def arrived(ref, sem):
         pltpu.make_async_copy(ref, ref, sem).wait()
 
+    z = c % NZ
     barrier = pltpu.get_barrier_semaphore()
-    partners = [dev(peer(*p), y, c) for p in PEERS] + [dev(me, other, c)]
-    partners += [dev(me, ny, hop(b)) for b in (1, 2, -1, -2) for ny in (y, other)]
-    for to in partners:
+    over = dev(me, other, c)
+    after = dev(me, (y + (z + 1) // NZ) % 2, hop(1))
+
+    def announce(to):
         pl.semaphore_signal(barrier, inc=1, device_id=to, device_id_type=MESH)
-    pl.semaphore_wait(barrier, len(partners))
+
+    for dx in range(1, NX):
+        announce(dev(((x + dx) % NX) * 2, y, c))
+
+    @pl.when(core == 1)
+    def _():
+        announce(dev(2 * x, y, c))
+
+    y_before, y_two = (y + 1 - (z + NZ - 1) // NZ) % 2, (y + (z + 2) // NZ) % 2
+    for ny, by in ((other, 0), ((y + (z + 1) // NZ) % 2, 1), (y_before, -1), (y_two, 2)):
+        announce(dev(2 * x + 1, ny, hop(by)))
+
+    def tell(sem):
+        pl.semaphore_signal(sem, inc=1, device_id=dev(2 * x + 1 - core, y, c), device_id_type=MESH)
+
+    @pl.when(core == 0)
+    def _():
+        pl.semaphore_wait(barrier, NJ - 1)
+        tell(met)
+
+    @pl.when(core == 1)
+    def _():
+        pl.semaphore_wait(met, 1)
 
     def kv_src(ref, j):
         return ref.at[:, 0, :, pl.ds(pl.multiple_of(j * HD, HD), HD)]
@@ -86,6 +110,12 @@
             pltpu.make_async_copy(q_src(ref, a, me), to.at[a, me], q_rs.at[n, a, me]).start()
 
     send_q(0)
+
+    def send_rest(a, _):
+        send_q(a)
+        return _
+
+    lax.fori_loop(1, SLOTS, send_rest, 0)
 
     doc = doc_ref[...]
     row = lax.broadcasted_iota(jnp.int32, doc.shape, 0)
@@ -104,55 +134,88 @@
     for n in range(2):
         for j in range(NJ):
             arrived(kv_dst(n, j), a_rs.at[n, j])
-    z = c % NZ
-    over, step = dev(me, other, c), (c + 1) // NCTX
-    after = dev(me, (y + (z + 1) // NZ) % 2, hop(1))
+    step = (c + 1) // NCTX
     halves = ((y + 1 - (z + NZ - 2) // NZ) % 2, (y + 1 - (z + NZ - 1) // NZ) % 2, y)
 
     def half(a, piece, of):
         return kv.at[:, a, piece, :, halves[of]]
 
-    def own_out(a):
+    for first, piece in ((0, 0), (0, 1), (1, 0)):
+
+        @pl.when(c == first)
+        def _(piece=piece):
+            kv[:, 0, piece] = jnp.zeros((2, NX, 2, GRP, HD), jnp.bfloat16)
+
+    def sends_near(a):
+        return (c < NCTX - 1) | (a < SLOTS - 1)
+
+    def has_near(a):
+        return (c > 0) | (a > 0)
+
+    def has_far(a):
+        return (c > 1) | (a > 0)
+
+    def own_over(a):
+        return remote(half(a, 2, 2), half(a, 2, 2), f_ss.at[a, 0], f_rs.at[a, 0], over)
+
+    def own_after(a):
         at = (a + step) % SLOTS
-        return (
-            remote(half(a, 2, 2), half(a, 2, 2), f_ss.at[a, 0], f_rs.at[a, 0], over),
-            remote(half(a, 2, 2), half(at, 1, 2), f_ss.at[a, 1], f_rs.at[at, 1], after),
-        )
-
-    def near_out(a):
+        return remote(half(a, 2, 2), half(at, 1, 2), f_ss.at[a, 1], f_rs.at[at, 1], after)
+
+    def near_after(a):
         at = (a + step) % SLOTS
-        return (
-            remote(half(a, 1, 1), half(at, 0, 1), f_ss.at[a, 3], f_rs.at[at, 3], after),
-            remote(half(a, 1, 1), half(a, 1, 1), f_ss.at[a, 2], f_rs.at[a, 2], over),
-        )
-
-    def far_out(a):
-        return (remote(half(a, 0, 0), half(a, 0, 0), f_ss.at[a, 4], f_rs.at[a, 4], over),)
-
-    def onward(copies, a, came=None):
-        if came is not None:
-            arrived(rx.at[a, 0], f_rs.at[a, came])
-        for copy in copies(a):
-            copy.start()
-
-    def own_slot(a, _):
-        onward(own_out, a)
-        return _
+        return remote(half(a, 1, 1), half(at, 0, 1), f_ss.at[a, 3], f_rs.at[at, 3], after)
+
+    def near_over(a):
+        return remote(half(a, 1, 1), half(a, 1, 1), f_ss.at[a, 2], f_rs.at[a, 2], over)
+
+    def far_over(a):
+        return remote(half(a, 0, 0), half(a, 0, 0), f_ss.at[a, 4], f_rs.at[a, 4], over)
+
+    def came(a, n):
+        arrived(rx.at[a, 0], f_rs.at[a, n])
+
+    @pl.when(core == 1)
+    def _():
+        pl.semaphore_wait(barrier, 8)
+        tell(met)
+
+    @pl.when(core == 0)
+    def _():
+        pl.semaphore_wait(met, 1)
+
+    def own_slot(a, carry):
+        @pl.when(sends_near(a))
+        def _():
+            own_after(a).start()
+
+        own_over(a).start()
+        return carry
 
     lax.fori_loop(0, SLOTS, own_slot, 0)
 
-    def send_rest(a, _):
-        send_q(a)
-        return _
-
-    lax.fori_loop(1, SLOTS, send_rest, 0)
-
-    def near_slot(a, _):
-        onward(near_out, a, 1)
-        return _
+    def near_slot(a, carry):
+        @pl.when(has_near(a))
+        def _():
+            came(a, 1)
+
+            @pl.when(sends_near(a))
+            def _():
+                near_after(a).start()
+
+            near_over(a).start()
+
+        return carry
 
     lax.fori_loop(0, SLOTS, near_slot, 0)
-    onward(far_out, 0, 3)
+
+    def far_slot(a):
+        @pl.when((a < SLOTS) & has_far(a))
+        def _():
+            came(a, 3)
+            far_over(a).start()
+
+    far_slot(0)
 
     key_at = lax.broadcasted_iota(jnp.int32, (NKEY, HD), 0)
     lane8 = lax.broadcasted_iota(jnp.int32, (8, HD), 1)
@@ -243,12 +306,17 @@
             owner_copy(a, piece).start()
 
     def slot(a, carry):
-        @pl.when(a < SLOTS - 1)
+        far_slot(a + 1)
+        came(a, 0)
+
+        @pl.when(has_near(a))
         def _():
-            onward(far_out, a + 1, 3)
-
-        for n in (0, 2, 4):
-            arrived(rx.at[a, 0], f_rs.at[a, n])
+            came(a, 2)
+
+        @pl.when(has_far(a))
+        def _():
+            came(a, 4)
+
         acc[...] = jnp.zeros_like(acc)
 
         def one(i, carry):
@@ -302,8 +370,13 @@
             for n, to in enumerate((qr, gr)):
                 arrived(to.at[a, j], q_ss.at[n, a, j])
             arrived(dqs.at[a, j], dq_ss.at[a, j])
+        def sent(n):
+            arrived(rx.at[a, 0], f_ss.at[a, n])
+
+        sent(0)
+        for n, when in ((1, sends_near(a)), (2, has_near(a)), (3, has_near(a) & sends_near(a)), (4, has_far(a))):
+            pl.when(when)(functools.partial(sent, n))
         for n in range(5):
-            arrived(rx.at[a, 0], f_ss.at[a, n])
             arrived(rx.at[a, 0], dk_ss.at[a, n])
         return _
 
@@ -319,12 +392,26 @@
                 arrived(home_src(n, 0, at), h_rs.at[part, n, j])
 
 
+def handed_on(dq, dk, dv, dq_out, dk_out, dv_out, dq_mid, dk_mid, dv_mid, sem):
+    parts = [(dq, dq_mid, dq_out, a) for a in range(SLOTS)]
+    parts += [(dk, dk_mid, dk_out, pl.ds(0, SLOTS)), (dv, dv_mid, dv_out, pl.ds(0, SLOTS))]
+    ins = [pltpu.make_async_copy(r.at[at], m.at[at], sem.at[0, n]) for n, (r, m, _, at) in enumerate(parts)]
+    outs = [pltpu.make_async_copy(m.at[at], o.at[at], sem.at[1, n]) for n, (_, m, o, at) in enumerate(parts)]
+    for copy in ins:
+        copy.start()
+    for one, two in zip(ins, outs):
+        one.wait()
+        two.start()
+    for copy in outs:
+        copy.wait()
+
+
 def body(queries, key_vectors, value_vectors, grad_output, doc_ids):
     bf, f32, dma = jnp.bfloat16, jnp.float32, pltpu.SemaphoreType.DMA
     hbm = pl.BlockSpec(memory_space=pltpu.HBM)
     vmem = pltpu.VMEM
     like = jax.ShapeDtypeStruct
-    return pl.pallas_call(
+    results = pl.pallas_call(
         kernel,
         out_shape=(
             like(queries.shape, bf),
@@ -363,11 +450,19 @@
             dma((SLOTS, 5)),
             dma((2, 2, NJ)),
             dma((2, 2, NJ)),
+            pltpu.SemaphoreType.REGULAR,
         ],
         compiler_params=pltpu.CompilerParams(
             collective_id=0, has_side_effects=True, vmem_limit_bytes=62 << 20
         ),
     )(queries, key_vectors, value_vectors, grad_output, doc_ids.reshape(HD, HD))
+    return pl.pallas_call(
+        handed_on,
+        out_shape=tuple(like(r.shape, bf) for r in results),
+        in_specs=[hbm] * 3,
+        out_specs=(hbm,) * 3,
+        scratch_shapes=[vmem(r.shape, bf) for r in results] + [dma((2, 6))],
+    )(*results)
 
 
 def solution(mesh):

time: 79.1 us -> 73.2 us (0.925); the launches traced: 78.9 us -> 72.1 us
  local copies, waits for them, and re-layouts: 4.01 us -> 0 us
  Pallas kernels: 74.2 us -> 71.4 us
    pallas_call x1, Pallas kernels: 74.2 us -> 69.1 us  [body(): pl.pallas_call(kernel, out_shape=(like(queries.shape, bf), like(key_vecto...]
    unnamed x7 -> x0, local copies, waits for them, and re-layouts: 4.01 us -> none
    pallas_call x0 -> x1, Pallas kernels: none -> 2.32 us  [body(): pl.pallas_call(handed_on, out_shape=tuple((like(r.shape, bf) for r in res...]
where the time goes in v3:
time: 73.2 us; the launch traced here: 72.1 us
  Pallas kernels  71.4 us (98%)
    pallas_call x1, Pallas kernels, body(): pl.pallas_call(kernel, out_shape=(like(queries.shape, bf), like(key_vecto...  69.1 us
    pallas_call x1, Pallas kernels, body(): pl.pallas_call(handed_on, out_shape=tuple((like(r.shape, bf) for r in res...  2.32 us

profile of v3, /device:TPU:1, one launch (start us, length us, event | category | flops | bytes accessed | tf_op | source)
XLA Modules:
  0.0 72.1 jit_solution(8694438868519256562)
XLA Ops:
  0.6 69.1 %shard_map.76 = (bf16[4,1,16,12288]{3,2,1,0:T(8,128)(2,1)}, bf16[4,1,16,1024]{3,2,1,0:T(8,128)(2,1)}, bf16[4,1,16,1024]{3,2,1,0:T(8,128)(2,1)}) custom-call(bf16[4,1,16,12288]{3,2,1,0:T(8,128)(2,1)} %q_ref.1, bf16[4,1,16,1024]{3,2,1,0:T(8,128)(2,1)} %k_ref.1, bf16[4,1,16,1024]{3,2,1,0:T(8,128)(2,1)} %v_ref.1, bf16[4,1,16,12288]{3,2,1,0:T(8,128)(2,1)} %g_ref.1, ...), custom_call_target="tpu_custom_call" | custom-call | tf_op jit(solution)/shard_map/pallas_call | solution.py:414
  69.7 2.3 %shard_map.77 = (bf16[4,1,16,12288]{3,2,1,0:T(8,128)(2,1)}, bf16[4,1,16,1024]{3,2,1,0:T(8,128)(2,1)}, bf16[4,1,16,1024]{3,2,1,0:T(8,128)(2,1)}) custom-call(bf16[4,1,16,12288]{3,2,1,0:T(8,128)(2,1)} %get-tuple-element.6.dq, bf16[4,1,16,1024]{3,2,1,0:T(8,128)(2,1)} %get-tuple-element.7.dk, bf16[4,1,16,1024]{3,2,1,0:T(8,128)(2,1)} %get-tuple-element.8.dv), custom_call_target="tpu_custom_call" | custom-call | tf_op jit(solution)/shard_map/pallas_call | solution.py:459

commit v4 on v3

--- a/solution.py
+++ b/solution.py
@@ -21,6 +21,7 @@
 QW = HPG * HD
 NKEY = 17 * GRP
 STACK = HPG * GRP
+HOLD = 2
 LOG2E = 1.4426950408889634
 FACTOR = 1.0 / math.sqrt(HD)
 PEERS = tuple((dx, dc) for dx in (2, 1, 3, 0) for dc in (0, 1) if (dx, dc) != (0, 0))
@@ -94,9 +95,9 @@
     for p in PEERS:
         j = peer(*p)
         for n, ref in enumerate((k_ref, v_ref)):
-            remote(kv_src(ref, j), kv_dst(n, me), a_ss.at[n, j], a_rs.at[n, me], dev(j, y, c)).start()
+            remote(kv_src(ref, j), kv_dst(n, me), a_ss.at[n], a_rs.at[n], dev(j, y, c)).start()
     for n, ref in enumerate((k_ref, v_ref)):
-        pltpu.make_async_copy(kv_src(ref, me), kv_dst(n, me), a_rs.at[n, me]).start()
+        pltpu.make_async_copy(kv_src(ref, me), kv_dst(n, me), a_rs.at[n]).start()
 
     def q_src(ref, a, j):
         return ref.at[a, 0, :, pl.ds(pl.multiple_of(j * QW, QW), QW)]
@@ -105,7 +106,7 @@
         for p in PEERS:
             j = peer(*p)
             for n, (ref, to) in enumerate(((q_ref, qr), (g_ref, gr))):
-                remote(q_src(ref, a, j), to.at[a, me], q_ss.at[n, a, j], q_rs.at[n, a, me], dev(j, y, c)).start()
+                remote(q_src(ref, a, j), to.at[a, me], q_ss.at[n], q_rs.at[n, a, me], dev(j, y, c)).start()
         for n, (ref, to) in enumerate(((q_ref, qr), (g_ref, gr))):
             pltpu.make_async_copy(q_src(ref, a, me), to.at[a, me], q_rs.at[n, a, me]).start()
 
@@ -132,8 +133,7 @@
     start[...] = jnp.maximum(run, carry)
 
     for n in range(2):
-        for j in range(NJ):
-            arrived(kv_dst(n, j), a_rs.at[n, j])
+        arrived(kv.at[n, :, 2, :, y], a_rs.at[n])
     step = (c + 1) // NCTX
     halves = ((y + 1 - (z + NZ - 2) // NZ) % 2, (y + 1 - (z + NZ - 1) // NZ) % 2, y)
 
@@ -224,11 +224,31 @@
     def dq_dst(a, j):
         return dq_ref.at[a, 0, :, pl.ds(pl.multiple_of(j * QW, QW), QW)]
 
+    def send_dq(a, xs):
+        for nc in range(2):
+            j = 2 * xs + nc
+
+            @pl.when(j == me)
+            def _(j=j):
+                pltpu.make_async_copy(dqs.at[a, j], dq_dst(a, me), dq_rs.at[0]).start()
+
+            @pl.when(j != me)
+            def _(j=j):
+                remote(dqs.at[a, j], dq_dst(a, me), dq_ss.at[0], dq_rs.at[0], dev(j, y, c)).start()
+
+    def held_dq():
+        def each(n, carry):
+            send_dq(n // NX, (x + 2 * (n % 2) + (n % NX) // 2) % NX)
+            return carry
+
+        lax.fori_loop(0, HOLD * NX + 1, each, 0)
+
     def chunk(a, i):
         xs = (x + 2 * (i % 2) + i // 2) % NX
         for nc in range(2):
             for n, to in enumerate((qr, gr)):
                 arrived(to.at[a, 2 * xs + nc], q_rs.at[n, a, 2 * xs + nc])
+        pl.when((a == HOLD) & (i == 1))(held_dq)
         off = 2 * xs + y
         for h in range(HPG):
             at = pl.ds(h * HD, HD)
@@ -270,16 +290,7 @@
         dq = (dq * FACTOR).astype(jnp.bfloat16)
         for h in range(HPG):
             dqs[a, pl.ds(2 * xs, 2), :, pl.ds(h * HD, HD)] = dq[h * GRP : (h + 1) * GRP].reshape(2, ROWS, HD)
-        for nc in range(2):
-            j = 2 * xs + nc
-
-            @pl.when(j == me)
-            def _():
-                pltpu.make_async_copy(dqs.at[a, j], dq_dst(a, me), dq_rs.at[a, me]).start()
-
-            @pl.when(j != me)
-            def _():
-                remote(dqs.at[a, j], dq_dst(a, me), dq_ss.at[a, j], dq_rs.at[a, me], dev(j, y, c)).start()
+        pl.when((a > HOLD) | ((a == HOLD) & (i > 0)))(functools.partial(send_dq, a, xs))
 
     def swap_copy(a, piece):
         return remote(dks.at[a, piece], rx.at[a, piece], dk_ss.at[a, piece], dk_rs.at[a, piece], over)
@@ -334,7 +345,20 @@
 
     lax.fori_loop(0, SLOTS, slot, 0)
 
-    pass_back(SLOTS - 1)
+    for n, to in enumerate((qr, gr)):
+        arrived(to.at[:, pl.ds(0, NJ - 1)], q_ss.at[n])
+        arrived(kc.at[pl.ds(0, (NJ - 1) * SLOTS * ROWS)], a_ss.at[n])
+
+    def sent_keys(a, carry):
+        def sent(n):
+            arrived(rx.at[a, 0], f_ss.at[a, n])
+
+        sent(0)
+        for n, when in ((1, sends_near(a)), (2, has_near(a)), (3, has_near(a) & sends_near(a)), (4, has_far(a))):
+            pl.when(when)(functools.partial(sent, n))
+        return carry
+
+    lax.fori_loop(0, SLOTS, sent_keys, 0)
 
     def reduce(a, _):
         for n in (2, 3, 4):
@@ -351,45 +375,31 @@
     def home_dst(n, j, at):
         return (dk_ref, dv_ref)[n].at[at, 0, :, pl.ds(pl.multiple_of(j * HD, HD), HD)]
 
-    for part, (low, many) in enumerate(((0, SLOTS - 1), (SLOTS - 1, 1))):
-        lax.fori_loop(low, low + many, reduce, 0)
-        at = pl.ds(low, many)
-        for n in range(2):
-            pltpu.make_async_copy(home_src(n, me, at), home_dst(n, me, at), h_rs.at[part, n, me]).start()
-            for p in PEERS:
-                j = peer(*p)
-                remote(
-                    home_src(n, j, at), home_dst(n, me, at), h_ss.at[part, n, j], h_rs.at[part, n, me], dev(j, y, c)
-                ).start()
-
-    def drain(a, _):
-        for j in range(NJ):
-            arrived(dqs.at[a, j], dq_rs.at[a, j])
+    def go_home(part):
+        lax.fori_loop(2 * part, 2 * part + 2, reduce, 0)
+        at = pl.ds(2 * part, 2)
         for p in PEERS:
             j = peer(*p)
-            for n, to in enumerate((qr, gr)):
-                arrived(to.at[a, j], q_ss.at[n, a, j])
-            arrived(dqs.at[a, j], dq_ss.at[a, j])
-        def sent(n):
-            arrived(rx.at[a, 0], f_ss.at[a, n])
-
-        sent(0)
-        for n, when in ((1, sends_near(a)), (2, has_near(a)), (3, has_near(a) & sends_near(a)), (4, has_far(a))):
-            pl.when(when)(functools.partial(sent, n))
+            for n in range(2):
+                remote(home_src(n, j, at), home_dst(n, me, at), h_ss.at[n], h_rs.at[n], dev(j, y, c)).start()
+        for n in range(2):
+            pltpu.make_async_copy(home_src(n, me, at), home_dst(n, me, at), h_rs.at[n]).start()
+
+    go_home(0)
+    pass_back(SLOTS - 1)
+    go_home(1)
+
+    def sent_grads(a, carry):
         for n in range(5):
             arrived(rx.at[a, 0], dk_ss.at[a, n])
-        return _
-
-    lax.fori_loop(0, SLOTS, drain, 0)
-    for n in range(2):
-        for p in PEERS:
-            j = peer(*p)
-            arrived(kv_dst(n, j), a_ss.at[n, j])
-        for part, at in enumerate((pl.ds(0, SLOTS - 1), pl.ds(SLOTS - 1, 1))):
-            for p in PEERS:
-                arrived(home_src(n, 0, at), h_ss.at[part, n, peer(*p)])
-            for j in range(NJ):
-                arrived(home_src(n, 0, at), h_rs.at[part, n, j])
+        return carry
+
+    lax.fori_loop(0, SLOTS, sent_grads, 0)
+    arrived(dqs.at[:, pl.ds(0, NJ - 1)], dq_ss.at[0])
+    arrived(dq_ref, dq_rs.at[0])
+    for n, ref in enumerate((dk_ref, dv_ref)):
+        arrived(kc.at[pl.ds(0, (NJ - 1) * SLOTS * ROWS)], h_ss.at[n])
+        arrived(ref, h_rs.at[n])
 
 
 def handed_on(dq, dk, dv, dq_out, dk_out, dv_out, dq_mid, dk_mid, dv_mid, sem):
@@ -438,18 +448,18 @@
             vmem((SLOTS, 2, 2, NX, GRP, HD), bf),
             vmem((SLOTS, 2, 2, NX, GRP, HD), bf),
             vmem((2, SLOTS, NX, GRP, HD), bf),
+            dma((2,)),
             dma((2, SLOTS, NJ)),
-            dma((2, SLOTS, NJ)),
-            dma((2, NJ)),
-            dma((2, NJ)),
+            dma((2,)),
+            dma((2,)),
             dma((SLOTS, 5)),
             dma((SLOTS, 5)),
-            dma((SLOTS, NJ)),
-            dma((SLOTS, NJ)),
+            dma((1,)),
+            dma((1,)),
             dma((SLOTS, 5)),
             dma((SLOTS, 5)),
-            dma((2, 2, NJ)),
-            dma((2, 2, NJ)),
+            dma((2,)),
+            dma((2,)),
             pltpu.SemaphoreType.REGULAR,
         ],
         compiler_params=pltpu.CompilerParams(

time: 73.2 us -> 71 us (0.970)
  Pallas kernels: 71.4 us -> 69.2 us
    pallas_call x1, Pallas kernels: 69.1 us -> 66.9 us  [body(): pl.pallas_call(kernel, out_shape=(like(queries.shape, bf), like(key_vecto...]
where the time goes in v4:
time: 71 us; the launch traced here: 69.9 us
  Pallas kernels  69.2 us (97%)
    pallas_call x1, Pallas kernels, body(): pl.pallas_call(kernel, out_shape=(like(queries.shape, bf), like(key_vecto...  66.9 us
    pallas_call x1, Pallas kernels, body(): pl.pallas_call(handed_on, out_shape=tuple((like(r.shape, bf) for r in res...  2.32 us

profile of v4, /device:TPU:1, one launch (start us, length us, event | category | flops | bytes accessed | tf_op | source)
XLA Modules:
  0.0 69.9 jit_solution(14632986738497188316)
XLA Ops:
  0.6 66.9 %shard_map.76 = (bf16[4,1,16,12288]{3,2,1,0:T(8,128)(2,1)}, bf16[4,1,16,1024]{3,2,1,0:T(8,128)(2,1)}, bf16[4,1,16,1024]{3,2,1,0:T(8,128)(2,1)}) custom-call(bf16[4,1,16,12288]{3,2,1,0:T(8,128)(2,1)} %q_ref.1, bf16[4,1,16,1024]{3,2,1,0:T(8,128)(2,1)} %k_ref.1, bf16[4,1,16,1024]{3,2,1,0:T(8,128)(2,1)} %v_ref.1, bf16[4,1,16,12288]{3,2,1,0:T(8,128)(2,1)} %g_ref.1, ...), custom_call_target="tpu_custom_call" | custom-call | tf_op jit(solution)/shard_map/pallas_call | solution.py:424
  67.5 2.3 %shard_map.77 = (bf16[4,1,16,12288]{3,2,1,0:T(8,128)(2,1)}, bf16[4,1,16,1024]{3,2,1,0:T(8,128)(2,1)}, bf16[4,1,16,1024]{3,2,1,0:T(8,128)(2,1)}) custom-call(bf16[4,1,16,12288]{3,2,1,0:T(8,128)(2,1)} %get-tuple-element.6.dq, bf16[4,1,16,1024]{3,2,1,0:T(8,128)(2,1)} %get-tuple-element.7.dk, bf16[4,1,16,1024]{3,2,1,0:T(8,128)(2,1)} %get-tuple-element.8.dv), custom_call_target="tpu_custom_call" | custom-call | tf_op jit(solution)/shard_map/pallas_call | solution.py:469

commit v5 on v4

--- a/solution.py
+++ b/solution.py
@@ -21,7 +21,7 @@
 QW = HPG * HD
 NKEY = 17 * GRP
 STACK = HPG * GRP
-HOLD = 2
+HOLD = 3
 LOG2E = 1.4426950408889634
 FACTOR = 1.0 / math.sqrt(HD)
 PEERS = tuple((dx, dc) for dx in (2, 1, 3, 0) for dc in (0, 1) if (dx, dc) != (0, 0))
@@ -241,14 +241,16 @@
             send_dq(n // NX, (x + 2 * (n % 2) + (n % NX) // 2) % NX)
             return carry
 
-        lax.fori_loop(0, HOLD * NX + 1, each, 0)
-
-    def chunk(a, i):
+        lax.fori_loop(0, HOLD * NX, each, 0)
+
+    def await_chunk(a, i):
         xs = (x + 2 * (i % 2) + i // 2) % NX
         for nc in range(2):
             for n, to in enumerate((qr, gr)):
                 arrived(to.at[a, 2 * xs + nc], q_rs.at[n, a, 2 * xs + nc])
-        pl.when((a == HOLD) & (i == 1))(held_dq)
+        return xs
+
+    def chunk(a, xs, qc, gc, kc, vc, bias):
         off = 2 * xs + y
         for h in range(HPG):
             at = pl.ds(h * HD, HD)
@@ -290,7 +292,14 @@
         dq = (dq * FACTOR).astype(jnp.bfloat16)
         for h in range(HPG):
             dqs[a, pl.ds(2 * xs, 2), :, pl.ds(h * HD, HD)] = dq[h * GRP : (h + 1) * GRP].reshape(2, ROWS, HD)
-        pl.when((a > HOLD) | ((a == HOLD) & (i > 0)))(functools.partial(send_dq, a, xs))
+
+    def pair(a, i):
+        both = [await_chunk(a, 2 * i), await_chunk(a, 2 * i + 1)]
+        pl.when((a == HOLD) & (i == 0))(held_dq)
+        for n, xs in enumerate(both):
+            chunk(a, xs, *[ref.at[n] for ref in (qc, gc, kc, vc, bias)])
+        for xs in both:
+            pl.when(a >= HOLD)(functools.partial(send_dq, a, xs))
 
     def swap_copy(a, piece):
         return remote(dks.at[a, piece], rx.at[a, piece], dk_ss.at[a, piece], dk_rs.at[a, piece], over)
@@ -331,15 +340,15 @@
         acc[...] = jnp.zeros_like(acc)
 
         def one(i, carry):
-            chunk(a, i)
-
-            @pl.when((i == 1) & (a > 0))
+            pair(a, i)
+
+            @pl.when((i == 0) & (a > 0))
             def _():
                 pass_back(a - 1)
 
             return carry
 
-        lax.fori_loop(0, NX, one, 0)
+        lax.fori_loop(0, NX // 2, one, 0)
         swap(a)
         return carry
 
@@ -347,7 +356,7 @@
 
     for n, to in enumerate((qr, gr)):
         arrived(to.at[:, pl.ds(0, NJ - 1)], q_ss.at[n])
-        arrived(kc.at[pl.ds(0, (NJ - 1) * SLOTS * ROWS)], a_ss.at[n])
+        arrived(kc.at[0, pl.ds(0, (NJ - 1) * SLOTS * ROWS)], a_ss.at[n])
 
     def sent_keys(a, carry):
         def sent(n):
@@ -398,7 +407,7 @@
     arrived(dqs.at[:, pl.ds(0, NJ - 1)], dq_ss.at[0])
     arrived(dq_ref, dq_rs.at[0])
     for n, ref in enumerate((dk_ref, dv_ref)):
-        arrived(kc.at[pl.ds(0, (NJ - 1) * SLOTS * ROWS)], h_ss.at[n])
+        arrived(kc.at[0, pl.ds(0, (NJ - 1) * SLOTS * ROWS)], h_ss.at[n])
         arrived(ref, h_rs.at[n])
 
 
@@ -435,11 +444,11 @@
             vmem((SLOTS, NJ, ROWS, QW), bf),
             vmem((SLOTS, NJ, ROWS, QW), bf),
             vmem((2, SLOTS, 3, NX, 2, GRP, HD), bf),
-            vmem((STACK, HD), bf),
-            vmem((STACK, HD), bf),
-            vmem((NKEY, HD), bf),
-            vmem((NKEY, HD), bf),
-            vmem((NKEY, HD), f32),
+            vmem((2, STACK, HD), bf),
+            vmem((2, STACK, HD), bf),
+            vmem((2, NKEY, HD), bf),
+            vmem((2, NKEY, HD), bf),
+            vmem((2, NKEY, HD), f32),
             vmem((HD, HD), jnp.int32),
             vmem((2, 24, GRP, HD), f32),
             vmem((SLOTS, 3, 2, NX, GRP, HD), bf),

time: 71 us -> 69.6 us (0.980); the launches traced: 69.9 us -> 69.3 us
  no operation moved by 1% of the time
where the time goes in v5:
time: 69.6 us; the launch traced here: 69.3 us
  Pallas kernels  68.7 us (99%)
    pallas_call x1, Pallas kernels, body(): pl.pallas_call(kernel, out_shape=(like(queries.shape, bf), like(key_vecto...  66.4 us
    pallas_call x1, Pallas kernels, body(): pl.pallas_call(handed_on, out_shape=tuple((like(r.shape, bf) for r in res...  2.32 us

profile of v5, /device:TPU:1, one launch (start us, length us, event | category | flops | bytes accessed | tf_op | source)
XLA Modules:
  0.0 69.3 jit_solution(12780926958974305395)
XLA Ops:
  0.6 66.4 %shard_map.76 = (bf16[4,1,16,12288]{3,2,1,0:T(8,128)(2,1)}, bf16[4,1,16,1024]{3,2,1,0:T(8,128)(2,1)}, bf16[4,1,16,1024]{3,2,1,0:T(8,128)(2,1)}) custom-call(bf16[4,1,16,12288]{3,2,1,0:T(8,128)(2,1)} %q_ref.1, bf16[4,1,16,1024]{3,2,1,0:T(8,128)(2,1)} %k_ref.1, bf16[4,1,16,1024]{3,2,1,0:T(8,128)(2,1)} %v_ref.1, bf16[4,1,16,12288]{3,2,1,0:T(8,128)(2,1)} %g_ref.1, ...), custom_call_target="tpu_custom_call" | custom-call | tf_op jit(solution)/shard_map/pallas_call | solution.py:433
  67.0 2.3 %shard_map.77 = (bf16[4,1,16,12288]{3,2,1,0:T(8,128)(2,1)}, bf16[4,1,16,1024]{3,2,1,0:T(8,128)(2,1)}, bf16[4,1,16,1024]{3,2,1,0:T(8,128)(2,1)}) custom-call(bf16[4,1,16,12288]{3,2,1,0:T(8,128)(2,1)} %get-tuple-element.6.dq, bf16[4,1,16,1024]{3,2,1,0:T(8,128)(2,1)} %get-tuple-element.7.dk, bf16[4,1,16,1024]{3,2,1,0:T(8,128)(2,1)} %get-tuple-element.8.dv), custom_call_target="tpu_custom_call" | custom-call | tf_op jit(solution)/shard_map/pallas_call | solution.py:478

commit v6 on v5

--- a/solution.py
+++ b/solution.py
@@ -21,7 +21,7 @@
 QW = HPG * HD
 NKEY = 17 * GRP
 STACK = HPG * GRP
-HOLD = 3
+HOLD = 2
 LOG2E = 1.4426950408889634
 FACTOR = 1.0 / math.sqrt(HD)
 PEERS = tuple((dx, dc) for dx in (2, 1, 3, 0) for dc in (0, 1) if (dx, dc) != (0, 0))
@@ -29,7 +29,7 @@
 
 def kernel(
     q_ref, k_ref, v_ref, g_ref, doc_ref, dq_ref, dk_ref, dv_ref,
-    qr, gr, dqs, kv, qc, gc, kc, vc, bias, start, acc, dks, dko, rx, dsum, own, home,
+    qr, gr, dqs, kv, qc, gc, kc, vc, bias, band, start, acc, dks, dko, rx, dsum, own, home,
     q_ss, q_rs, a_ss, a_rs, f_ss, f_rs, dq_ss, dq_rs, dk_ss, dk_rs, h_ss, h_rs, met,
 ):
     head = lax.axis_index("head")
@@ -112,11 +112,88 @@
 
     send_q(0)
 
-    def send_rest(a, _):
-        send_q(a)
-        return _
-
-    lax.fori_loop(1, SLOTS, send_rest, 0)
+    send_q(1)
+
+    for n in range(2):
+        arrived(kv.at[n, :, 2, :, y], a_rs.at[n])
+    step = (c + 1) // NCTX
+    halves = ((y + 1 - (z + NZ - 2) // NZ) % 2, (y + 1 - (z + NZ - 1) // NZ) % 2, y)
+
+    def half(a, piece, of):
+        return kv.at[:, a, piece, :, halves[of]]
+
+    for first, piece in ((0, 0), (0, 1), (1, 0)):
+
+        @pl.when(c == first)
+        def _(piece=piece):
+            kv[:, 0, piece] = jnp.zeros((2, NX, 2, GRP, HD), jnp.bfloat16)
+
+    def sends_near(a):
+        return (c < NCTX - 1) | (a < SLOTS - 1)
+
+    def has_near(a):
+        return (c > 0) | (a > 0)
+
+    def has_far(a):
+        return (c > 1) | (a > 0)
+
+    def own_over(a):
+        return remote(half(a, 2, 2), half(a, 2, 2), f_ss.at[a, 0], f_rs.at[a, 0], over)
+
+    def own_after(a):
+        at = (a + step) % SLOTS
+        return remote(half(a, 2, 2), half(at, 1, 2), f_ss.at[a, 1], f_rs.at[at, 1], after)
+
+    def near_after(a):
+        at = (a + step) % SLOTS
+        return remote(half(a, 1, 1), half(at, 0, 1), f_ss.at[a, 3], f_rs.at[at, 3], after)
+
+    def near_over(a):
+        return remote(half(a, 1, 1), half(a, 1, 1), f_ss.at[a, 2], f_rs.at[a, 2], over)
+
+    def far_over(a):
+        return remote(half(a, 0, 0), half(a, 0, 0), f_ss.at[a, 4], f_rs.at[a, 4], over)
+
+    def came(a, n):
+        arrived(rx.at[a, 0], f_rs.at[a, n])
+
+    @pl.when(core == 1)
+    def _():
+        pl.semaphore_wait(barrier, 8)
+        tell(met)
+
+    @pl.when(core == 0)
+    def _():
+        pl.semaphore_wait(met, 1)
+
+    def own_slot(a):
+        @pl.when(sends_near(a))
+        def _():
+            own_after(a).start()
+
+        own_over(a).start()
+
+    def near_slot(a):
+        @pl.when(has_near(a))
+        def _():
+            came(a, 1)
+
+            @pl.when(sends_near(a))
+            def _():
+                near_after(a).start()
+
+            near_over(a).start()
+
+    def far_slot(a):
+        @pl.when((a < SLOTS) & has_far(a))
+        def _():
+            came(a, 3)
+            far_over(a).start()
+
+    own_slot(0)
+    own_slot(1)
+    send_q(2)
+    send_q(3)
 
     doc = doc_ref[...]
     row = lax.broadcasted_iota(jnp.int32, doc.shape, 0)
@@ -132,94 +209,16 @@
         carry = jnp.maximum(carry, jnp.where(row >= s, pltpu.roll(carry, s, 0), 0))
     start[...] = jnp.maximum(run, carry)
 
-    for n in range(2):
-        arrived(kv.at[n, :, 2, :, y], a_rs.at[n])
-    step = (c + 1) // NCTX
-    halves = ((y + 1 - (z + NZ - 2) // NZ) % 2, (y + 1 - (z + NZ - 1) // NZ) % 2, y)
-
-    def half(a, piece, of):
-        return kv.at[:, a, piece, :, halves[of]]
-
-    for first, piece in ((0, 0), (0, 1), (1, 0)):
-
-        @pl.when(c == first)
-        def _(piece=piece):
-            kv[:, 0, piece] = jnp.zeros((2, NX, 2, GRP, HD), jnp.bfloat16)
-
-    def sends_near(a):
-        return (c < NCTX - 1) | (a < SLOTS - 1)
-
-    def has_near(a):
-        return (c > 0) | (a > 0)
-
-    def has_far(a):
-        return (c > 1) | (a > 0)
-
-    def own_over(a):
-        return remote(half(a, 2, 2), half(a, 2, 2), f_ss.at[a, 0], f_rs.at[a, 0], over)
-
-    def own_after(a):
-        at = (a + step) % SLOTS
-        return remote(half(a, 2, 2), half(at, 1, 2), f_ss.at[a, 1], f_rs.at[at, 1], after)
-
-    def near_after(a):
-        at = (a + step) % SLOTS
-        return remote(half(a, 1, 1), half(at, 0, 1), f_ss.at[a, 3], f_rs.at[at, 3], after)
-
-    def near_over(a):
-        return remote(half(a, 1, 1), half(a, 1, 1), f_ss.at[a, 2], f_rs.at[a, 2], over)
-
-    def far_over(a):
-        return remote(half(a, 0, 0), half(a, 0, 0), f_ss.at[a, 4], f_rs.at[a, 4], over)
-
-    def came(a, n):
-        arrived(rx.at[a, 0], f_rs.at[a, n])
-
-    @pl.when(core == 1)
-    def _():
-        pl.semaphore_wait(barrier, 8)
-        tell(met)
-
-    @pl.when(core == 0)
-    def _():
-        pl.semaphore_wait(met, 1)
-
-    def own_slot(a, carry):
-        @pl.when(sends_near(a))
-        def _():
-            own_after(a).start()
-
-        own_over(a).start()
-        return carry
-
-    lax.fori_loop(0, SLOTS, own_slot, 0)
-
-    def near_slot(a, carry):
-        @pl.when(has_near(a))
-        def _():
-            came(a, 1)
-
-            @pl.when(sends_near(a))
-            def _():
-                near_after(a).start()
-
-            near_over(a).start()
-
-        return carry
-
-    lax.fori_loop(0, SLOTS, near_slot, 0)
-
-    def far_slot(a):
-        @pl.when((a < SLOTS) & has_far(a))
-        def _():
-            came(a, 3)
-            far_over(a).start()
-
+    near_slot(0)
+    own_slot(2)
+    near_slot(1)
     far_slot(0)
+    own_slot(3)
 
     key_at = lax.broadcasted_iota(jnp.int32, (NKEY, HD), 0)
     lane8 = lax.broadcasted_iota(jnp.int32, (8, HD), 1)
-    row_in = lane8 % GRP
+    ahead = key_at - lax.broadcasted_iota(jnp.int32, (NKEY, HD), 1) % GRP
+    band[...] = jnp.where((ahead > 0) & (ahead <= 512), 0.0, -1e30)
 
     def dq_dst(a, j):
         return dq_ref.at[a, 0, :, pl.ds(pl.multiple_of(j * QW, QW), QW)]
@@ -266,9 +265,7 @@
         line = jnp.where(lane8 < GRP, line, 0)
         line = line + pltpu.roll(line, GRP, 1)
         line = line + pltpu.roll(line, 2 * GRP, 1)
-        low = jnp.maximum(line - (first - 512), row_in + 1)[:1]
-        high = (row_in + 512)[:1]
-        bias[...] = jnp.where((key_at >= low) & (key_at <= high), 0.0, -1e30)
+        bias[...] = jnp.where(key_at >= (line - (first - 512))[:1], band[...], -1e30)
         nt = (((1,), (1,)), ((), ()))
         scores = lax.dot_general(kc[...], qc[...], nt, preferred_element_type=jnp.float32)
         dweights = lax.dot_general(vc[...], gc[...], nt, preferred_element_type=jnp.float32)
@@ -326,7 +323,6 @@
             owner_copy(a, piece).start()
 
     def slot(a, carry):
-        far_slot(a + 1)
         came(a, 0)
 
         @pl.when(has_near(a))
@@ -341,6 +337,14 @@
 
         def one(i, carry):
             pair(a, i)
+
+            @pl.when(i == 0)
+            def _():
+                far_slot(a + 1)
+
+            @pl.when(a == 0)
+            def _():
+                near_slot(2 + i)
 
             @pl.when((i == 0) & (a > 0))
             def _():
@@ -449,6 +453,7 @@
             vmem((2, NKEY, HD), bf),
             vmem((2, NKEY, HD), bf),
             vmem((2, NKEY, HD), f32),
+            vmem((NKEY, HD), f32),
             vmem((HD, HD), jnp.int32),
             vmem((2, 24, GRP, HD), f32),
             vmem((SLOTS, 3, 2, NX, GRP, HD), bf),

time: 69.6 us -> 69.3 us (level)
  no operation moved by 1% of the time
where the time goes in v6:
time: 69.3 us; the launch traced here: 69.1 us
  Pallas kernels  68.5 us (99%)
    pallas_call x1, Pallas kernels, body(): pl.pallas_call(kernel, out_shape=(like(queries.shape, bf), like(key_vecto...  66.1 us
    pallas_call x1, Pallas kernels, body(): pl.pallas_call(handed_on, out_shape=tuple((like(r.shape, bf) for r in res...  2.32 us

profile of v6, /device:TPU:1, one launch (start us, length us, event | category | flops | bytes accessed | tf_op | source)
XLA Modules:
  0.0 69.1 jit_solution(4583758225871719937)
XLA Ops:
  0.6 66.1 %shard_map.76 = (bf16[4,1,16,12288]{3,2,1,0:T(8,128)(2,1)}, bf16[4,1,16,1024]{3,2,1,0:T(8,128)(2,1)}, bf16[4,1,16,1024]{3,2,1,0:T(8,128)(2,1)}) custom-call(bf16[4,1,16,12288]{3,2,1,0:T(8,128)(2,1)} %q_ref.1, bf16[4,1,16,1024]{3,2,1,0:T(8,128)(2,1)} %k_ref.1, bf16[4,1,16,1024]{3,2,1,0:T(8,128)(2,1)} %v_ref.1, bf16[4,1,16,12288]{3,2,1,0:T(8,128)(2,1)} %g_ref.1, ...), custom_call_target="tpu_custom_call" | custom-call | tf_op jit(solution)/shard_map/pallas_call | solution.py:437
  66.8 2.3 %shard_map.77 = (bf16[4,1,16,12288]{3,2,1,0:T(8,128)(2,1)}, bf16[4,1,16,1024]{3,2,1,0:T(8,128)(2,1)}, bf16[4,1,16,1024]{3,2,1,0:T(8,128)(2,1)}) custom-call(bf16[4,1,16,12288]{3,2,1,0:T(8,128)(2,1)} %get-tuple-element.6.dq, bf16[4,1,16,1024]{3,2,1,0:T(8,128)(2,1)} %get-tuple-element.7.dk, bf16[4,1,16,1024]{3,2,1,0:T(8,128)(2,1)} %get-tuple-element.8.dv), custom_call_target="tpu_custom_call" | custom-call | tf_op jit(solution)/shard_map/pallas_call | solution.py:483

commit v7 on v6

--- a/solution.py
+++ b/solution.py
@@ -74,126 +74,20 @@
     for ny, by in ((other, 0), ((y + (z + 1) // NZ) % 2, 1), (y_before, -1), (y_two, 2)):
         announce(dev(2 * x + 1, ny, hop(by)))
 
-    def tell(sem):
-        pl.semaphore_signal(sem, inc=1, device_id=dev(2 * x + 1 - core, y, c), device_id_type=MESH)
-
-    @pl.when(core == 0)
-    def _():
-        pl.semaphore_wait(barrier, NJ - 1)
-        tell(met)
-
-    @pl.when(core == 1)
-    def _():
-        pl.semaphore_wait(met, 1)
-
     def kv_src(ref, j):
         return ref.at[:, 0, :, pl.ds(pl.multiple_of(j * HD, HD), HD)]
 
     def kv_dst(n, j):
         return kv.at[n, :, 2, j // 2, y, pl.ds(pl.multiple_of((j % 2) * ROWS, ROWS), ROWS)]
 
-    for p in PEERS:
-        j = peer(*p)
-        for n, ref in enumerate((k_ref, v_ref)):
-            remote(kv_src(ref, j), kv_dst(n, me), a_ss.at[n], a_rs.at[n], dev(j, y, c)).start()
+    def q_src(ref, a, j):
+        return ref.at[a, 0, :, pl.ds(pl.multiple_of(j * QW, QW), QW)]
+
     for n, ref in enumerate((k_ref, v_ref)):
         pltpu.make_async_copy(kv_src(ref, me), kv_dst(n, me), a_rs.at[n]).start()
-
-    def q_src(ref, a, j):
-        return ref.at[a, 0, :, pl.ds(pl.multiple_of(j * QW, QW), QW)]
-
-    def send_q(a):
-        for p in PEERS:
-            j = peer(*p)
-            for n, (ref, to) in enumerate(((q_ref, qr), (g_ref, gr))):
-                remote(q_src(ref, a, j), to.at[a, me], q_ss.at[n], q_rs.at[n, a, me], dev(j, y, c)).start()
+    for a in range(SLOTS):
         for n, (ref, to) in enumerate(((q_ref, qr), (g_ref, gr))):
             pltpu.make_async_copy(q_src(ref, a, me), to.at[a, me], q_rs.at[n, a, me]).start()
-
-    send_q(0)
-
-    send_q(1)
-
-    for n in range(2):
-        arrived(kv.at[n, :, 2, :, y], a_rs.at[n])
-    step = (c + 1) // NCTX
-    halves = ((y + 1 - (z + NZ - 2) // NZ) % 2, (y + 1 - (z + NZ - 1) // NZ) % 2, y)
-
-    def half(a, piece, of):
-        return kv.at[:, a, piece, :, halves[of]]
-
-    for first, piece in ((0, 0), (0, 1), (1, 0)):
-
-        @pl.when(c == first)
-        def _(piece=piece):
-            kv[:, 0, piece] = jnp.zeros((2, NX, 2, GRP, HD), jnp.bfloat16)
-
-    def sends_near(a):
-        return (c < NCTX - 1) | (a < SLOTS - 1)
-
-    def has_near(a):
-        return (c > 0) | (a > 0)
-
-    def has_far(a):
-        return (c > 1) | (a > 0)
-
-    def own_over(a):
-        return remote(half(a, 2, 2), half(a, 2, 2), f_ss.at[a, 0], f_rs.at[a, 0], over)
-
-    def own_after(a):
-        at = (a + step) % SLOTS
-        return remote(half(a, 2, 2), half(at, 1, 2), f_ss.at[a, 1], f_rs.at[at, 1], after)
-
-    def near_after(a):
-        at = (a + step) % SLOTS
-        return remote(half(a, 1, 1), half(at, 0, 1), f_ss.at[a, 3], f_rs.at[at, 3], after)
-
-    def near_over(a):
-        return remote(half(a, 1, 1), half(a, 1, 1), f_ss.at[a, 2], f_rs.at[a, 2], over)
-
-    def far_over(a):
-        return remote(half(a, 0, 0), half(a, 0, 0), f_ss.at[a, 4], f_rs.at[a, 4], over)
-
-    def came(a, n):
-        arrived(rx.at[a, 0], f_rs.at[a, n])
-
-    @pl.when(core == 1)
-    def _():
-        pl.semaphore_wait(barrier, 8)
-        tell(met)
-
-    @pl.when(core == 0)
-    def _():
-        pl.semaphore_wait(met, 1)
-
-    def own_slot(a):
-        @pl.when(sends_near(a))
-        def _():
-            own_after(a).start()
-
-        own_over(a).start()
-
-    def near_slot(a):
-        @pl.when(has_near(a))
-        def _():
-            came(a, 1)
-
-            @pl.when(sends_near(a))
-            def _():
-                near_after(a).start()
-
-            near_over(a).start()
-
-    def far_slot(a):
-        @pl.when((a < SLOTS) & has_far(a))
-        def _():
-            came(a, 3)
-            far_over(a).start()
-
-    own_slot(0)
-    own_slot(1)
-    send_q(2)
-    send_q(3)
 
     doc = doc_ref[...]
     row = lax.broadcasted_iota(jnp.int32, doc.shape, 0)
@@ -209,16 +103,125 @@
         carry = jnp.maximum(carry, jnp.where(row >= s, pltpu.roll(carry, s, 0), 0))
     start[...] = jnp.maximum(run, carry)
 
+    key_at = lax.broadcasted_iota(jnp.int32, (NKEY, HD), 0)
+    ahead = key_at - lax.broadcasted_iota(jnp.int32, (NKEY, HD), 1) % GRP
+    band[...] = jnp.where((ahead > 0) & (ahead <= 512), 0.0, -1e30)
+
+    for first, piece in ((0, 0), (0, 1), (1, 0)):
+
+        @pl.when(c == first)
+        def _(piece=piece):
+            kv[:, 0, piece] = jnp.zeros((2, NX, 2, GRP, HD), jnp.bfloat16)
+
+    def tell(sem):
+        pl.semaphore_signal(sem, inc=1, device_id=dev(2 * x + 1 - core, y, c), device_id_type=MESH)
+
+    @pl.when(core == 0)
+    def _():
+        pl.semaphore_wait(barrier, NJ - 1)
+        tell(met)
+
+    @pl.when(core == 1)
+    def _():
+        pl.semaphore_wait(met, 1)
+
+    for p in PEERS:
+        j = peer(*p)
+        for n, ref in enumerate((k_ref, v_ref)):
+            remote(kv_src(ref, j), kv_dst(n, me), a_ss.at[n], a_rs.at[n], dev(j, y, c)).start()
+
+    def send_q(a):
+        for p in PEERS:
+            j = peer(*p)
+            for n, (ref, to) in enumerate(((q_ref, qr), (g_ref, gr))):
+                remote(q_src(ref, a, j), to.at[a, me], q_ss.at[n], q_rs.at[n, a, me], dev(j, y, c)).start()
+
+    send_q(0)
+
+    send_q(1)
+
+    for n in range(2):
+        arrived(kv.at[n, :, 2, :, y], a_rs.at[n])
+    step = (c + 1) // NCTX
+    halves = ((y + 1 - (z + NZ - 2) // NZ) % 2, (y + 1 - (z + NZ - 1) // NZ) % 2, y)
+
+    def half(a, piece, of):
+        return kv.at[:, a, piece, :, halves[of]]
+
+    def sends_near(a):
+        return (c < NCTX - 1) | (a < SLOTS - 1)
+
+    def has_near(a):
+        return (c > 0) | (a > 0)
+
+    def has_far(a):
+        return (c > 1) | (a > 0)
+
+    def own_over(a):
+        return remote(half(a, 2, 2), half(a, 2, 2), f_ss.at[a, 0], f_rs.at[a, 0], over)
+
+    def own_after(a):
+        at = (a + step) % SLOTS
+        return remote(half(a, 2, 2), half(at, 1, 2), f_ss.at[a, 1], f_rs.at[at, 1], after)
+
+    def near_after(a):
+        at = (a + step) % SLOTS
+        return remote(half(a, 1, 1), half(at, 0, 1), f_ss.at[a, 3], f_rs.at[at, 3], after)
+
+    def near_over(a):
+        return remote(half(a, 1, 1), half(a, 1, 1), f_ss.at[a, 2], f_rs.at[a, 2], over)
+
+    def far_over(a):
+        return remote(half(a, 0, 0), half(a, 0, 0), f_ss.at[a, 4], f_rs.at[a, 4], over)
+
+    def came(a, n):
+        arrived(rx.at[a, 0], f_rs.at[a, n])
+
+    @pl.when(core == 1)
+    def _():
+        pl.semaphore_wait(barrier, 8)
+        tell(met)
+
+    @pl.when(core == 0)
+    def _():
+        pl.semaphore_wait(met, 1)
+
+    def own_slot(a):
+        @pl.when(sends_near(a))
+        def _():
+            own_after(a).start()
+
+        own_over(a).start()
+
+    def near_slot(a):
+        @pl.when(has_near(a))
+        def _():
+            came(a, 1)
+
+            @pl.when(sends_near(a))
+            def _():
+                near_after(a).start()
+
+            near_over(a).start()
+
+    def far_slot(a):
+        @pl.when((a < SLOTS) & has_far(a))
+        def _():
+            came(a, 3)
+            far_over(a).start()
+
+    own_slot(0)
+    own_slot(1)
+    send_q(2)
+    send_q(3)
+
     near_slot(0)
     own_slot(2)
     near_slot(1)
     far_slot(0)
     own_slot(3)
 
-    key_at = lax.broadcasted_iota(jnp.int32, (NKEY, HD), 0)
     lane8 = lax.broadcasted_iota(jnp.int32, (8, HD), 1)
-    ahead = key_at - lax.broadcasted_iota(jnp.int32, (NKEY, HD), 1) % GRP
-    band[...] = jnp.where((ahead > 0) & (ahead <= 512), 0.0, -1e30)
 
     def dq_dst(a, j):
         return dq_ref.at[a, 0, :, pl.ds(pl.multiple_of(j * QW, QW), QW)]

time: 69.3 us -> 69.3 us (level)
  no operation moved by 1% of the time
where the time goes in v7:
time: 69.3 us; the launch traced here: 69.1 us
  Pallas kernels  68.5 us (99%)
    pallas_call x1, Pallas kernels, body(): pl.pallas_call(kernel, out_shape=(like(queries.shape, bf), like(key_vecto...  66.1 us
    pallas_call x1, Pallas kernels, body(): pl.pallas_call(handed_on, out_shape=tuple((like(r.shape, bf) for r in res...  2.32 us

profile of v7, /device:TPU:1, one launch (start us, length us, event | category | flops | bytes accessed | tf_op | source)
XLA Modules:
  0.0 69.1 jit_solution(10813895121222206039)
XLA Ops:
  0.6 66.1 %shard_map.76 = (bf16[4,1,16,12288]{3,2,1,0:T(8,128)(2,1)}, bf16[4,1,16,1024]{3,2,1,0:T(8,128)(2,1)}, bf16[4,1,16,1024]{3,2,1,0:T(8,128)(2,1)}) custom-call(bf16[4,1,16,12288]{3,2,1,0:T(8,128)(2,1)} %q_ref.1, bf16[4,1,16,1024]{3,2,1,0:T(8,128)(2,1)} %k_ref.1, bf16[4,1,16,1024]{3,2,1,0:T(8,128)(2,1)} %v_ref.1, bf16[4,1,16,12288]{3,2,1,0:T(8,128)(2,1)} %g_ref.1, ...), custom_call_target="tpu_custom_call" | custom-call | tf_op jit(solution)/shard_map/pallas_call | solution.py:440
  66.8 2.3 %shard_map.77 = (bf16[4,1,16,12288]{3,2,1,0:T(8,128)(2,1)}, bf16[4,1,16,1024]{3,2,1,0:T(8,128)(2,1)}, bf16[4,1,16,1024]{3,2,1,0:T(8,128)(2,1)}) custom-call(bf16[4,1,16,12288]{3,2,1,0:T(8,128)(2,1)} %get-tuple-element.6.dq, bf16[4,1,16,1024]{3,2,1,0:T(8,128)(2,1)} %get-tuple-element.7.dk, bf16[4,1,16,1024]{3,2,1,0:T(8,128)(2,1)} %get-tuple-element.8.dv), custom_call_target="tpu_custom_call" | custom-call | tf_op jit(solution)/shard_map/pallas_call | solution.py:486

commit v8 on v6

--- a/solution.py
+++ b/solution.py
@@ -237,7 +237,7 @@
 
     def held_dq():
         def each(n, carry):
-            send_dq(n // NX, (x + 2 * (n % 2) + (n % NX) // 2) % NX)
+            send_dq(n % HOLD, (x + 2 + 3 * (n // HOLD)) % NX)
             return carry
 
         lax.fori_loop(0, HOLD * NX, each, 0)

time: 69.3 us -> 69.2 us (level)
  no operation moved by 1% of the time
where the time goes in v8:
time: 69.2 us; the launch traced here: 69.1 us
  Pallas kernels  68.4 us (99%)
    pallas_call x1, Pallas kernels, body(): pl.pallas_call(kernel, out_shape=(like(queries.shape, bf), like(key_vecto...  66.1 us
    pallas_call x1, Pallas kernels, body(): pl.pallas_call(handed_on, out_shape=tuple((like(r.shape, bf) for r in res...  2.32 us

profile of v8, /device:TPU:1, one launch (start us, length us, event | category | flops | bytes accessed | tf_op | source)
XLA Modules:
  0.0 69.1 jit_solution(1426850544790434672)
XLA Ops:
  0.6 66.1 %shard_map.76 = (bf16[4,1,16,12288]{3,2,1,0:T(8,128)(2,1)}, bf16[4,1,16,1024]{3,2,1,0:T(8,128)(2,1)}, bf16[4,1,16,1024]{3,2,1,0:T(8,128)(2,1)}) custom-call(bf16[4,1,16,12288]{3,2,1,0:T(8,128)(2,1)} %q_ref.1, bf16[4,1,16,1024]{3,2,1,0:T(8,128)(2,1)} %k_ref.1, bf16[4,1,16,1024]{3,2,1,0:T(8,128)(2,1)} %v_ref.1, bf16[4,1,16,12288]{3,2,1,0:T(8,128)(2,1)} %g_ref.1, ...), custom_call_target="tpu_custom_call" | custom-call | tf_op jit(solution)/shard_map/pallas_call | solution.py:437
  66.7 2.3 %shard_map.77 = (bf16[4,1,16,12288]{3,2,1,0:T(8,128)(2,1)}, bf16[4,1,16,1024]{3,2,1,0:T(8,128)(2,1)}, bf16[4,1,16,1024]{3,2,1,0:T(8,128)(2,1)}) custom-call(bf16[4,1,16,12288]{3,2,1,0:T(8,128)(2,1)} %get-tuple-element.6.dq, bf16[4,1,16,1024]{3,2,1,0:T(8,128)(2,1)} %get-tuple-element.7.dk, bf16[4,1,16,1024]{3,2,1,0:T(8,128)(2,1)} %get-tuple-element.8.dv), custom_call_target="tpu_custom_call" | custom-call | tf_op jit(solution)/shard_map/pallas_call | solution.py:483
